TPU v7x, 256 devices: a whole 4x4x8 slice. The times are simulated.
256 devices in a mesh: vocab: 16 (over x_lo, y, core), seq: 8 (over z), grp: 2 (over x_hi).
Axes of the slice: x: 4 (x_hi: 2, x_lo: 2; x = x_hi * 2 + x_lo), y: 4, z: 8, core: 2. Of those that a mesh axis runs over, the one named last changes fastest.
Arguments:
- decoder_states: bfloat16 [1024, 2048], P('seq'), may hold values from -64 to 64
- encoder_states: bfloat16 [2048, 2048], P(('seq', 'grp')), may hold values from -256 to 256
- ln_gains: float32 [2, 2048], replicated, may hold values from 0.5 to 1.5
- w_query: bfloat16 [2048, 2048], P(None, 'vocab'), may hold values from -0.13258252 to 0.13258252
- w_key: bfloat16 [2048, 2048], P(None, 'vocab'), may hold values from -0.13258252 to 0.13258252
- w_value: bfloat16 [2048, 2048], P(None, 'vocab'), may hold values from -0.125 to 0.125
- w_out: bfloat16 [2048, 2048], P('vocab'), may hold values from -5 to 5
- embedding: bfloat16 [229376, 2048], P(('vocab', 'seq', 'grp')), may hold values from -2 to 2
- labels: int32 [1024], replicated, may hold values from 0 to 229375
- src_length: int32 [1], replicated, may hold values from 1024 to 2048
- tgt_length: int32 [1], replicated, may hold values from 512 to 1024
Outputs:
- token_loss: float32 [1024], replicated
- grad_table: bfloat16 [229376, 2048], P(('vocab', 'seq', 'grp'))
All inputs are finite; a program needn't handle non-finite values.
Results may differ from a plain program's by a relative error of at most 0.0082.
Values may be sent and summed in bfloat16 or wider, within the bound.
A program may use at most 64 MiB of HBM per device.

v0:
```python
import math

import jax
import jax.numpy as jnp
from jax import lax
from jax.sharding import PartitionSpec as P

HEAD_DIM = 128


EPSILON = 1e-05


def layer_norm(matrix, gain_row):
    row_mean = jnp.mean(matrix, axis=-1, keepdims=True)
    centred = matrix - row_mean
    variance = jnp.mean(centred * centred, axis=-1, keepdims=True)
    return centred * lax.rsqrt(variance + EPSILON) * gain_row


def body(
    decoder_states,
    encoder_states,
    ln_gains,
    w_query,
    w_key,
    w_value,
    w_out,
    embedding,
    labels,
    src_length,
    tgt_length,
):
    head_width = HEAD_DIM
    local_heads = w_query.shape[1] // head_width
    row_count = decoder_states.shape[0]
    states = decoder_states.astype(jnp.float32)
    normed = layer_norm(states, ln_gains[0]).astype(jnp.bfloat16)
    query_scale = 1.0 / math.sqrt(head_width)
    query = (jnp.dot(normed, w_query, preferred_element_type=jnp.float32) * query_scale).astype(
        jnp.bfloat16
    )
    key_rows = jnp.dot(encoder_states, w_key, preferred_element_type=jnp.float32).astype(
        jnp.bfloat16
    )
    value_rows = jnp.dot(encoder_states, w_value, preferred_element_type=jnp.float32).astype(
        jnp.bfloat16
    )
    key_rows, value_rows = (
        lax.all_gather(key_rows, ("seq", "grp"), axis=0, tiled=True),
        lax.all_gather(value_rows, ("seq", "grp"), axis=0, tiled=True),
    )
    source_count = key_rows.shape[0]
    key_valid = jnp.arange(source_count) < src_length[0]
    scores = jnp.einsum(
        "qhd,khd->hqk",
        query.reshape(row_count, local_heads, head_width),
        key_rows.reshape(source_count, local_heads, head_width),
        preferred_element_type=jnp.float32,
    )
    scores = jnp.where(key_valid[None, None, :], scores, -1e30)
    score_top = jnp.max(scores, axis=2, keepdims=True)
    exp_scores = jnp.where(key_valid[None, None, :], jnp.exp(scores - score_top), 0.0)
    weights = (exp_scores / jnp.sum(exp_scores, axis=2, keepdims=True)).astype(jnp.bfloat16)
    context = jnp.einsum(
        "hqk,khd->qhd",
        weights,
        value_rows.reshape(source_count, local_heads, head_width),
        preferred_element_type=jnp.float32,
    )
    context = context.reshape(row_count, local_heads * head_width).astype(jnp.bfloat16)
    partial_out = jnp.dot(context, w_out, preferred_element_type=jnp.float32)
    target_count = labels.shape[0]
    positions = jnp.arange(target_count)
    attention = lax.psum(partial_out, "vocab")
    final_rows = layer_norm(states + attention, ln_gains[1]).astype(jnp.bfloat16)
    gathered = lax.all_gather(final_rows, "seq", axis=0, tiled=True)
    row_live = positions < tgt_length[0]
    table_rows = embedding.shape[0]
    table_base = lax.axis_index(("vocab", "seq", "grp")) * table_rows
    logits = lax.dot_general(
        gathered, embedding, (((1,), (1,)), ((), ())), preferred_element_type=jnp.float32
    )
    label_hit = labels[:, None] == table_base + jnp.arange(table_rows)[None, :]
    local_pick = jnp.sum(jnp.where(label_hit, logits, 0.0), axis=1)
    local_top = jnp.max(logits, axis=1)
    row_max = lax.pmax(local_top, ("vocab", "seq", "grp"))
    exp_logits = jnp.exp(logits - row_max[:, None])
    row_total, picked = lax.psum((jnp.sum(exp_logits, axis=1), local_pick), ("vocab", "seq", "grp"))
    prob_scale = 1.0 / row_total
    row_loss = jnp.where(row_live, row_max + jnp.log(row_total) - picked, 0.0)
    token_loss = jnp.zeros((target_count,), jnp.float32).at[positions].set(row_loss)
    grad_logits = jnp.where(
        row_live[:, None], exp_logits * prob_scale[:, None] - label_hit.astype(jnp.float32), 0.0
    ).astype(jnp.bfloat16)
    grad_table = lax.dot_general(
        grad_logits, gathered, (((0,), (0,)), ((), ())), preferred_element_type=jnp.float32
    ).astype(jnp.bfloat16)
    return (token_loss, grad_table)


def solution(mesh):
    in_specs = (
        P("seq", None),
        P(("seq", "grp"), None),
        P(),
        P(None, "vocab"),
        P(None, "vocab"),
        P(None, "vocab"),
        P("vocab", None),
        P(("vocab", "seq", "grp"), None),
        P(),
        P(),
        P(),
    )
    out_specs = (P(), P(("vocab", "seq", "grp"), None))
    return jax.shard_map(body, mesh=mesh, in_specs=in_specs, out_specs=out_specs, check_vma=False)
```

profile of v0, /device:TPU:1, one launch (start us, length us, event | category | flops | bytes accessed | tf_op | source)
XLA Modules:
  0.0 469.0 jit_solution(15561577848467336043)
XLA Ops:
  7.2 0.0 all-reduce.3.cloned.1.call-start
  7.2 0.8 fusion.45
  8.1 1.5 convolution_convert_fusion.3
  9.6 40.7 %all_gather.9 = bf16[2048,128]{1,0:T(8,128)(2,1)S(1)} all-gather(bf16[128,128]{1,0:T(8,128)(2,1)S(1)} %convolution_convert_fusion.3), channel_id=1, replica_groups=mesh['vocab'=16,'seq'=8,'grp'=2] {'seq','grp'}, dimensions={0}, use_global_device_ids=true | all-gather | bytes 557056 | tf_op jit(solution)/shard_map/all_gather | solution.py:51
  50.3 1.5 convolution_convert_fusion.2
  51.8 31.9 %all_gather.10 = bf16[2048,128]{1,0:T(8,128)(2,1)S(1)} all-gather(bf16[128,128]{1,0:T(8,128)(2,1)S(1)} %convolution_convert_fusion.2), channel_id=1, replica_groups=mesh['vocab'=16,'seq'=8,'grp'=2] {'seq','grp'}, dimensions={0}, use_global_device_ids=true | all-gather | bytes 557056 | tf_op jit(solution)/shard_map/all_gather | solution.py:50
  83.8 1.2 convert_reduce_fusion
  85.0 0.3 fusion.17
  85.9 0.7 fusion.46
  86.6 0.3 fusion.20
  87.0 2.9 fusion.16
  89.9 0.0 all-gather.2.cloned.1.call-start
  90.0 136.5 %all-reduce.3.cloned.1.call-done = f32[128,2048]{1,0:T(8,128)} async-done(((f32[128,2048]{1,0:T(8,128)}), f32[128,2048]{1,0:T(8,128)}) %all-reduce.3.cloned.1.call-update) | async-done | bytes 1048592 | tf_op jit(solution)/shard_map/psum | solution.py:75
  226.4 1.5 fusion.37
  227.9 1.5 multiply_reduce_fusion
  229.5 1.0 multiply_convert_fusion
  230.5 0.0 all-gather.2.cloned.1.call-update
  231.2 55.5 %all-gather.2.cloned.1.call-done = bf16[1024,2048]{1,0:T(8,128)(2,1)} async-done(((bf16[128,2048]{1,0:T(8,128)(2,1)}), bf16[1024,2048]{1,0:T(8,128)(2,1)}) %all-gather.2.cloned.1.call-update) | async-done | bytes 4194320 | tf_op jit(solution)/shard_map/all_gather | solution.py:77
  286.7 9.1 %fusion.49 = (f32[1024]{0:T(1024)S(1)}, f32[1024,896]{0,1:T(8,128)}) fusion(bf16[1024,2048]{1,0:T(8,128)(2,1)} %all-gather.2.cloned.1.call-done, bf16[896,2048]{1,0:T(8,128)(2,1)} %param.18), kind=kOutput, calls=%fused_computation.62 | convolution fusion | flops 3759012864 | bytes 11538432 | tf_op jit(solution)/shard_map/dot_general | solution.py:81
  295.8 76.4 %pmax.7 = f32[1024]{0:T(1024)S(1)} all-reduce(f32[1024]{0:T(1024)S(1)} %get-tuple-element.12), channel_id=1, replica_groups=mesh['vocab'=16,'seq'=8,'grp'=2] {'vocab','seq','grp'}, use_global_device_ids=true, to_apply=%region_8.9 | all-reduce | flops 1024 | bytes 8192 | tf_op jit(solution)/shard_map/pmax | solution.py:87
  372.2 2.9 fusion.4
  375.1 72.7 %all-reduce = (f32[1024]{0:T(1024)S(1)}, f32[1024]{0:T(1024)S(1)}) all-reduce(f32[1024]{0:T(1024)S(1)} %get-tuple-element.3, f32[1024]{0:T(1024)S(1)} %get-tuple-element.2), channel_id=1, replica_groups=mesh['vocab'=16,'seq'=8,'grp'=2] {'vocab','seq','grp'}, use_global_device_ids=true, to_apply=%region_12.13 | all-reduce | flops 2048 | bytes 16384 | tf_op jit(solution)/shard_map/psum | solution.py:89
  447.8 4.9 %scatter_custom_fusion = f32[1024]{0:T(1024)} fusion(s32[1024]{0:T(1024)S(1)} %iota.22, f32[1024]{0:T(1024)S(1)} %get-tuple-element.9, f32[]{:T(128)} %constant.14.clone.1), kind=kCustom, calls=%fused_computation.51 | custom fusion | bytes 4100 | tf_op jit(solution)/shard_map/scatter | solution.py:92
  452.7 9.5 %convolution_convert_fusion = bf16[896,2048]{1,0:T(8,128)(2,1)} fusion(bf16[1024,2048]{1,0:T(8,128)(2,1)} %all-gather.2.cloned.1.call-done, f32[1024,896]{0,1:T(8,128)} %get-tuple-element.13, f32[1024]{0:T(1024)S(1)} %get-tuple-element.8, s32[1024]{0:T(1024)S(1)} %copy-done.3, f32[1024]{0:T(1024)S(1)} %pmax.7, s32[896]{0:T(1024)S(1)} %iota_add_fusion, ...), kind=kOutput, calls=%fused_computation.8 | convolution fusion | flops 3766353920 | bytes 11551232 | tf_op jit(solution)/shard_map/dot_general | solution.py:96
  (18 shorter events, 0.1 us)
Async XLA Ops:
  7.2 78.8 %copy-start = (bf16[2048,128]{1,0:T(8,128)(2,1)S(1)}, bf16[2048,128]{1,0:T(8,128)(2,1)}, u32[]{:S(2)}) copy-start(bf16[2048,128]{1,0:T(8,128)(2,1)} %param.14) | copy-start | bytes 1572868
  7.2 77.8 %copy-start.1 = (bf16[128,2048]{1,0:T(8,128)(2,1)S(1)}, bf16[128,2048]{1,0:T(8,128)(2,1)}, u32[]{:S(2)}) copy-start(bf16[128,2048]{1,0:T(8,128)(2,1)} %param.11) | copy-start | bytes 1572868
  7.2 219.2 %all-reduce.3.cloned.1.call-start = ((), (), s32[]{:S(2)}) async-start(), calls=%async_computation | async-start | bytes 2097152 | tf_op jit(solution)/shard_map/psum | solution.py:75
  89.9 196.8 %all-gather.2.cloned.1.call-start = ((), (), s32[]{:S(2)}) async-start(), calls=%async_computation.1 | async-start | bytes 4718592 | tf_op jit(solution)/shard_map/all_gather | solution.py:77
  226.4 3.0 copy-start.2
  231.2 141.0 %copy-start.3 = (s32[1024]{0:T(1024)S(1)}, s32[1024]{0:T(1024)}, u32[]{:S(2)}) copy-start(s32[1024]{0:T(1024)} %param.19) | copy-start | bytes 12292
Sparse Core Ops, SparseCore 0:
  90.0 136.3 all-reduce.2
  230.6 56.0 all-gather.1
where the time goes:
time: 470 us; the launch traced here: 469 us
  blocking collectives  222 us (47%)
  waiting for transfers between devices  192 us (41%)
  matrix products  25.2 us (5%)
  between operations  15.4 us (3%)
  other arithmetic  8.79 us (2%)
  local copies, waits for them, and re-layouts  5.75 us (1%)
    psum x1, waiting for transfers between devices, body(): attention = lax.psum(partial_out, 'vocab')  136 us
    pmax x1, blocking collectives, body(): row_max = lax.pmax(local_top, ('vocab', 'seq', 'grp'))  76.4 us
    psum x1, blocking collectives, body(): lax.psum((jnp.sum(exp_logits, axis=1), local_pick), ('vocab', 'seq', 'grp'))  72.7 us
    all_gather x1, waiting for transfers between devices, body(): gathered = lax.all_gather(final_rows, 'seq', axis=0, tiled=True)  55.5 us
    all_gather x1, blocking collectives, body(): lax.all_gather(value_rows, ('seq', 'grp'), axis=0, tiled=True)  40.7 us
    all_gather x1, blocking collectives, body(): lax.all_gather(key_rows, ('seq', 'grp'), axis=0, tiled=True)  31.9 us
    dot_general x1, matrix products, body(): lax.dot_general(grad_logits, gathered, (((0,), (0,)), ((), ())), preferre...  9.47 us
  transfers between devices with their start and end apart: 2, of which 2 were waited for; matrix products, arithmetic and copies ran while one was open for 0% of the time, Pallas kernels for 0%

commit v1 on v0

v1 whole, which is shorter than its diff:
```python
import functools
import math

import jax
import jax.numpy as jnp
from jax import lax
from jax.experimental import pallas as pl
from jax.experimental.pallas import tpu as pltpu
from jax.sharding import PartitionSpec as P

HEAD_DIM = 128
EPSILON = 1e-05
MESH = pl.DeviceIdType.MESH
NC = 2
NY = 4
NT = (((1,), (1,)), ((), ()))
F32, BF16 = jnp.float32, jnp.bfloat16


def front_kernel(
    cfg,
    dec_in,
    enc_in,
    gains,
    labels,
    src_len,
    tgt_len,
    wq_in,
    wk_in,
    wv_in,
    wo_in,
    emb_in,
    loss_out,
    lse_out,
    hit_out,
    logit_out,
    rows_out,
    dec,
    enc,
    wq,
    wkv,
    wo,
    emb,
    kv,
    ctx_own,
    ctx_got,
    part,
    summed,
    norm_stat,
    rows,
    logit,
    local_stat,
    stat_x,
    stat_y,
    stat_z,
    load_sem,
    store_sem,
    kv_send,
    kv_recv,
    ctx_sem,
    sum_send,
    sum_recv,
    norm_send,
    norm_recv,
    first_send,
    first_recv,
    second_send,
    second_recv,
    ring_send,
    ring_recv,
    third_send,
    third_recv,
    core_send,
    core_recv,
    stat_send,
    stat_recv,
):
    nv, nz, ng, ny, nxl = cfg
    d = dec.shape[1]
    tz = dec.shape[0]
    ez = enc.shape[0]
    hd = wq.shape[1]
    tg = tz // ng
    ty = tg // ny
    width = d // (nxl * NC)
    wa, wb = width // 2, width // 4
    table_rows = emb.shape[0]
    nx = ng * nxl
    half = nz // 2

    v = lax.axis_index("vocab")
    z = lax.axis_index("seq")
    g = lax.axis_index("grp")
    c = v % NC
    y = (v // NC) % ny
    xl = v // (NC * ny)
    x = g * nxl + xl

    def vocab_of(xl_, y_, c_):
        return (xl_ * ny + y_) * NC + c_

    def at_x(x_, c_=None):
        return {"vocab": vocab_of(x_ % nxl, y, c if c_ is None else c_), "seq": z, "grp": x_ // nxl}

    def at_y(y_):
        return {"vocab": vocab_of(xl, y_, c), "seq": z, "grp": g}

    def at_z(z_):
        return {"vocab": v, "seq": z_, "grp": g}

    def at_v(v_):
        return {"vocab": v_, "seq": z, "grp": g}

    barrier = pltpu.get_barrier_semaphore()
    friends = [at_v((v + o) % nv) for o in range(1, nv)]
    friends += [at_z((z + o) % nz) for o in range(1, nz)]
    friends += [
        {"vocab": vocab_of(xl_, y, c_), "seq": z, "grp": (g + o) % ng}
        for o in range(1, ng)
        for xl_ in range(nxl)
        for c_ in range(NC)
    ]
    for friend in friends:
        pl.semaphore_signal(barrier, inc=1, device_id=friend, device_id_type=MESH)

    loads = [
        pltpu.make_async_copy(src, dst, load_sem.at[i])
        for i, (src, dst) in enumerate(
            (
                (enc_in, enc),
                (wk_in, wkv.at[:, 0:hd]),
                (wv_in, wkv.at[:, hd : 2 * hd]),
                (dec_in, dec),
                (wq_in, wq),
                (wo_in, wo),
                (emb_in, emb),
            )
        )
    ]
    for load in loads:
        load.start()

    sent = []

    def send(ref, dst, send_sem, recv_sem, device):
        copy = pltpu.make_async_remote_copy(
            src_ref=ref,
            dst_ref=dst,
            send_sem=send_sem,
            recv_sem=recv_sem,
            device_id=device,
            device_id_type=MESH,
        )
        copy.start()
        sent.append(copy)

    def arrived(ref, recv_sem):
        pltpu.make_async_remote_copy(
            src_ref=ref,
            dst_ref=ref,
            send_sem=load_sem.at[0],
            recv_sem=recv_sem,
            device_id=at_z((z + 1) % nz),
            device_id_type=MESH,
        ).wait_recv()

    def ring_post(view, t, send_sems, recv_sems):
        for way, step in ((0, 1), (1, nz - 1)):
            block = (z + t * (nz - step)) % nz
            for part_ in (0, 1) if t + 1 < half else (way,):
                ref = view(block, part_)
                send(ref, ref, send_sems.at[way, t, part_], recv_sems.at[way, t, part_], at_z((z + step) % nz))

    def ring_wait(view, t, recv_sems):
        for way, step in ((0, 1), (1, nz - 1)):
            block = (z + t * (nz - step)) % nz
            for part_ in (0, 1) if t < half else (way,):
                arrived(view(block, part_), recv_sems.at[way, t - 1, part_])

    def ring_blocks(t):
        return [(z + nz - t) % nz, (z + t) % nz] if t < half else [(z + half) % nz]

    for i in (0, 1, 2):
        loads[i].wait()
    own_kv = jnp.dot(enc[...], wkv[...], preferred_element_type=F32).astype(BF16)
    kv[z, 0] = own_kv[:, 0:hd]
    kv[z, 1] = own_kv[:, hd : 2 * hd]
    pl.semaphore_wait(barrier, len(friends))

    def kv_view(block, part_):
        return kv.at[block, part_]

    ring_post(kv_view, 0, kv_send, kv_recv)

    loads[3].wait()
    states = dec[...].astype(F32)
    centred = states - jnp.mean(states, axis=1, keepdims=True)
    variance = jnp.mean(centred * centred, axis=1, keepdims=True)
    normed = (centred * lax.rsqrt(variance + EPSILON) * gains[0:1, :]).astype(BF16)
    loads[4].wait()
    query = (jnp.dot(normed, wq[...], preferred_element_type=F32) * (1.0 / math.sqrt(hd))).astype(BF16)

    source_count = src_len[0]

    def scores_of(block):
        s = lax.dot_general(query, kv[block, 0], NT, preferred_element_type=F32)
        place = (block * ng + g) * ez + lax.broadcasted_iota(jnp.int32, s.shape, 1)
        valid = place < source_count
        return block, valid, jnp.where(valid, s, -1e30)

    scored = [scores_of(z)]
    for t in range(1, half + 1):
        ring_wait(kv_view, t, kv_recv)
        if t < half:
            ring_post(kv_view, t, kv_send, kv_recv)
        scored += [scores_of(block) for block in ring_blocks(t)]
    top = functools.reduce(jnp.maximum, [s for _, _, s in scored])
    top = jnp.max(top, axis=1, keepdims=True)
    total = jnp.zeros((tz, ez), F32)
    acc = jnp.zeros((tz, hd), F32)
    for block, valid, s in scored:
        e = jnp.where(valid, jnp.exp(s - top), 0.0)
        total = total + e
        acc = acc + jnp.dot(e.astype(BF16), kv[block, 1], preferred_element_type=F32)
    total = jnp.sum(total, axis=1, keepdims=True)
    low = lax.broadcasted_iota(jnp.int32, (tz, 128), 1) < 64
    ctx_own[:, 0:hd] = acc
    ctx_own[:, hd : hd + 128] = jnp.where(low, top, total)
    send(
        ctx_own.at[pl.ds(pl.multiple_of((1 - g) * tg, tg), tg)],
        ctx_got,
        ctx_sem.at[0],
        ctx_sem.at[1],
        {"vocab": v, "seq": z, "grp": 1 - g},
    )
    arrived(ctx_got, ctx_sem.at[1])
    mine = ctx_own[pl.ds(pl.multiple_of(g * tg, tg), tg), :]
    other = ctx_got[...]
    top0, top1 = mine[:, hd : hd + 1], other[:, hd : hd + 1]
    both = jnp.maximum(top0, top1)
    f0, f1 = jnp.exp(top0 - both), jnp.exp(top1 - both)
    total = mine[:, hd + 64 : hd + 65] * f0 + other[:, hd + 64 : hd + 65] * f1
    context = ((mine[:, 0:hd] * f0 + other[:, 0:hd] * f1) / total).astype(BF16)

    def columns_of(xl_, c_):
        base = c_ * (d // NC)
        return (
            (base + xl_ * wa, wa),
            (base + nxl * wa + xl_ * wb, wb),
            (base + nxl * (wa + wb) + xl_ * wb, wb),
        )

    loads[5].wait()
    projected = jnp.dot(context, wo[...], preferred_element_type=F32)
    for xl_ in range(nxl):
        for y_ in range(ny):
            for c_ in range(NC):
                at = 0
                for start, size in columns_of(xl_, c_):
                    part[vocab_of(xl_, y_, c_), :, at : at + size] = projected[
                        y_ * ty : (y_ + 1) * ty, start : start + size
                    ]
                    at += size
    for o in range(1, nv):
        to = (v + o) % nv
        send(part.at[to], summed.at[v], sum_send.at[o], sum_recv.at[v], at_v(to))
    own_cols = [(pl.multiple_of(start, 128), size) for start, size in columns_of(xl, c)]
    own_row = pl.multiple_of(g * tg + y * ty, ty)
    hidden = part[v] + jnp.concatenate(
        [dec[pl.ds(own_row, ty), pl.ds(start, size)].astype(F32) for start, size in own_cols], axis=1
    )
    for o in range(1, nv):
        frm = (v + o) % nv
        arrived(summed.at[frm], sum_recv.at[frm])
        hidden = hidden + summed[frm]

    piece = xl * NC + c
    pieces = nxl * NC
    own_mean = jnp.mean(hidden, axis=1, keepdims=True)
    own_square = jnp.sum((hidden - own_mean) * (hidden - own_mean), axis=1, keepdims=True)
    low = lax.broadcasted_iota(jnp.int32, (ty, 128), 1) < 64
    norm_stat[piece] = jnp.where(low, own_mean, own_square)
    for o in range(1, pieces):
        to = (piece + o) % pieces
        send(
            norm_stat.at[piece],
            norm_stat.at[piece],
            norm_send.at[o],
            norm_recv.at[piece],
            at_v(vocab_of(to // NC, y, to % NC)),
        )
    for o in range(1, pieces):
        frm = (piece + o) % pieces
        arrived(norm_stat.at[frm], norm_recv.at[frm])
    means = [norm_stat[i, :, 0:1] for i in range(pieces)]
    squares = [norm_stat[i, :, 64:65] for i in range(pieces)]
    mean = sum(means) * (1.0 / pieces)
    square = sum(squares) + width * sum((m - mean) * (m - mean) for m in means)
    scale = lax.rsqrt(square * (1.0 / d) + EPSILON)
    gain = jnp.concatenate([gains[1:2, pl.ds(start, size)] for start, size in own_cols], axis=1)
    final = ((hidden - mean) * scale * gain).astype(BF16)
    at = 0
    for start, size in own_cols:
        rows[z, g, y, :, pl.ds(start, size)] = final[:, at : at + size]
        at += size

    def cols_all(c_):
        base = pl.multiple_of(c_ * (d // NC), 128)
        return (
            pl.ds(base, nxl * wa),
            pl.ds(pl.multiple_of(base + nxl * wa, 128), nxl * wb),
            pl.ds(pl.multiple_of(base + nxl * (wa + wb), 128), nxl * wb),
        )

    def cols_piece(xl_):
        return [pl.ds(pl.multiple_of(start, 128), size) for start, size in columns_of(xl_, c)]

    own_a, own_b, own_c = cols_piece(xl)
    all_a, all_b, all_c = cols_all(c)

    def exchange(n, me, ref_of, send_sems, recv_sems, device_of):
        for o in range(1, n):
            ref = ref_of(me)
            send(ref, ref, send_sems.at[o], recv_sems.at[me], device_of((me + o) % n))

    def collect(n, me, ref_of, recv_sems, then=None):
        for o in range(1, n):
            frm = (me + o) % n
            arrived(ref_of(frm), recv_sems.at[frm])
            if then is not None:
                then(frm)

    def a1(x_):
        return rows.at[z, x_ // nxl, y, :, cols_piece(x_ % nxl)[0]]

    def b1(z_):
        return rows.at[z_, g, y, :, own_b]

    def c1(z_):
        return rows.at[z_, g, y, :, own_c]

    def a2(y_):
        return rows.at[z, :, y_, :, all_a]

    def b2(x_):
        return rows.at[:, x_ // nxl, y, :, cols_piece(x_ % nxl)[1]]

    def c2(y_):
        return rows.at[:, g, y_, :, own_c]

    def b3(y_):
        return rows.at[:, :, y_, :, all_b]

    def c3(x_):
        return rows.at[:, x_ // nxl, :, :, cols_piece(x_ % nxl)[2]]

    def a3(block, part_):
        base = pl.multiple_of(c * (d // NC) + part_ * (nxl * wa // 2), 128)
        return rows.at[block, :, :, :, pl.ds(base, nxl * wa // 2)]

    exchange(nx, x, a1, first_send.at[0], first_recv.at[0], at_x)
    exchange(nz, z, b1, first_send.at[1], first_recv.at[1], at_z)
    exchange(nz, z, c1, first_send.at[2], first_recv.at[2], at_z)
    collect(nx, x, a1, first_recv.at[0])
    exchange(ny, y, a2, second_send.at[0], second_recv.at[0], at_y)
    collect(nz, z, b1, first_recv.at[1])
    exchange(nx, x, b2, second_send.at[1], second_recv.at[1], at_x)
    collect(nz, z, c1, first_recv.at[2])
    exchange(ny, y, c2, second_send.at[2], second_recv.at[2], at_y)

    sibling = at_x(x, 1 - c)

    def to_core(kind, i, ref):
        send(ref, ref, core_send.at[kind, i], core_recv.at[kind, i], sibling)

    def a_block(c_):
        return lambda z_: rows.at[z_, :, :, :, cols_all(c_)[0]]

    def b_block(c_):
        return lambda y_: rows.at[:, :, y_, :, cols_all(c_)[1]]

    def c_block(c_):
        def view(x_):
            base = pl.multiple_of(c_ * (d // NC) + nxl * (wa + wb) + (x_ % nxl) * wb, 128)
            return rows.at[:, x_ // nxl, :, :, pl.ds(base, wb)]

        return view

    def share(kind, view):
        return lambda i: to_core(kind, i, view(c)(i))

    share_a, share_b, share_c = share(0, a_block), share(1, b_block), share(2, c_block)

    collect(ny, y, a2, second_recv.at[0])
    ring_post(a3, 0, ring_send, ring_recv)
    share_a(z)
    collect(nx, x, b2, second_recv.at[1])
    exchange(ny, y, b3, third_send.at[0], third_recv.at[0], at_y)
    share_b(y)
    collect(ny, y, c2, second_recv.at[2])
    exchange(nx, x, c3, third_send.at[1], third_recv.at[1], at_x)
    share_c(x)
    for t in range(1, half + 1):
        ring_wait(a3, t, ring_recv)
        if t < half:
            ring_post(a3, t, ring_send, ring_recv)
        for block in ring_blocks(t):
            share_a(block)
        if t == half - 1:
            collect(ny, y, b3, third_recv.at[0], share_b)
            collect(nx, x, c3, third_recv.at[1], share_c)
    for kind, count, view in ((0, nz, a_block), (1, ny, b_block), (2, nx, c_block)):
        for i in range(count):
            arrived(view(1 - c)(i), core_recv.at[kind, i])

    rows_store = pltpu.make_async_copy(rows, rows_out, store_sem.at[0])
    rows_store.start()

    loads[6].wait()
    table_base = ((v * nz + z) * ng + g) * table_rows
    step_blocks = max(1, 256 // tz)
    step_rows = step_blocks * tz

    def logit_step(i, carry):
        chunk = rows[pl.ds(i * step_blocks, step_blocks)].reshape(step_rows, d)
        lanes = pl.ds(pl.multiple_of(i * step_rows, 128), step_rows)
        values = lax.dot_general(emb[...], chunk, NT, preferred_element_type=F32)
        logit[:, lanes] = values
        top_ = jnp.max(values, axis=0, keepdims=True)
        total_ = jnp.sum(jnp.exp(values - top_), axis=0, keepdims=True)
        token = table_base + lax.broadcasted_iota(jnp.int32, values.shape, 0)
        local_stat[i, 0:1, :] = top_ + jnp.log(total_)
        local_stat[i, 1:2, :] = jnp.sum(jnp.where(token == labels[:, lanes], values, 0.0), axis=0, keepdims=True)
        return carry

    steps = nz // step_blocks
    lax.fori_loop(0, steps, logit_step, 0)
    logit_store = pltpu.make_async_copy(logit, logit_out, store_sem.at[1])
    logit_store.start()

    stat_rows = nz * tz // 128
    per_step = step_rows // 128
    nxc = nx * NC
    xc = x * NC + c
    for r in range(stat_rows):
        for k in range(2):
            stat_x[xc, k * stat_rows + r : k * stat_rows + r + 1, :] = local_stat[
                r // per_step, k : k + 1, (r % per_step) * 128 : (r % per_step + 1) * 128
            ]

    def merge(ref, n):
        lses = [ref[i, 0:stat_rows] for i in range(n)]
        top_ = functools.reduce(jnp.maximum, lses)
        total_ = sum(jnp.exp(s - top_) for s in lses)
        return top_ + jnp.log(total_), sum(ref[i, stat_rows : 2 * stat_rows] for i in range(n))

    def stat_round(ref, n, me, k, device_of):
        exchange(n, me, lambda i: ref.at[i], stat_send.at[k], stat_recv.at[k], device_of)
        collect(n, me, lambda i: ref.at[i], stat_recv.at[k])
        return merge(ref, n)

    lse, picked = stat_round(stat_x, nxc, xc, 0, lambda i: at_x(i // NC, i % NC))
    stat_y[y, 0:stat_rows] = lse
    stat_y[y, stat_rows : 2 * stat_rows] = picked
    lse, picked = stat_round(stat_y, ny, y, 1, at_y)
    stat_z[z, 0:stat_rows] = lse
    stat_z[z, stat_rows : 2 * stat_rows] = picked
    lse, picked = stat_round(stat_z, nz, z, 2, at_z)

    place = lax.broadcasted_iota(jnp.int32, lse.shape, 0) * 128 + lax.broadcasted_iota(jnp.int32, lse.shape, 1)
    live = place < tgt_len[0]
    loss_out[...] = jnp.where(live, lse - picked, 0.0)
    lse = jnp.where(live, lse, 1e30)
    for r in range(stat_rows):
        lse_out[0:1, r * 128 : (r + 1) * 128] = lse[r : r + 1, :]
    place = lax.broadcasted_iota(jnp.int32, labels.shape, 1)
    hit_out[...] = jnp.where(place < tgt_len[0], labels[...] - table_base, -1)

    for copy in sent:
        copy.wait_send()
    rows_store.wait()
    logit_store.wait()


def grad_kernel(lse, hit, logit, rows, out):
    base = pl.program_id(0) * out.shape[0]
    token = base + lax.broadcasted_iota(jnp.int32, logit.shape, 0)
    grad = jnp.exp(logit[...] - lse[...]) - jnp.where(token == hit[...], 1.0, 0.0)
    out[...] = jnp.dot(grad.astype(BF16), rows[...], preferred_element_type=F32).astype(BF16)


def body(
    cfg,
    decoder_states,
    encoder_states,
    ln_gains,
    w_query,
    w_key,
    w_value,
    w_out,
    embedding,
    labels,
    src_length,
    tgt_length,
):
    nv, nz, ng, ny, nxl = cfg
    tz, d = decoder_states.shape
    ez = encoder_states.shape[0]
    hd = w_query.shape[1]
    table_rows = embedding.shape[0]
    target = labels.shape[0]
    tg = tz // ng
    ty = tg // ny
    width = d // (nxl * NC)
    nx = ng * nxl
    half = nz // 2
    pieces = nxl * NC
    step_blocks = max(1, 256 // tz)
    stat_rows = target // 128
    most = max(nz, nx, ny)
    hbm = pl.BlockSpec(memory_space=pl.ANY)
    vmem = pl.BlockSpec(memory_space=pltpu.VMEM)
    smem = pl.BlockSpec(memory_space=pltpu.SMEM)
    dma = pltpu.SemaphoreType.DMA
    loss, lse, hit, logit, rows = pl.pallas_call(
        functools.partial(front_kernel, cfg),
        out_shape=(
            jax.ShapeDtypeStruct((stat_rows, 128), F32),
            jax.ShapeDtypeStruct((1, target), F32),
            jax.ShapeDtypeStruct((1, target), jnp.int32),
            jax.ShapeDtypeStruct((table_rows, target), F32),
            jax.ShapeDtypeStruct((nz, ng, ny, ty, d), BF16),
        ),
        in_specs=[hbm, hbm, vmem, vmem, smem, smem, hbm, hbm, hbm, hbm, hbm],
        out_specs=(vmem, vmem, vmem, hbm, hbm),
        scratch_shapes=[
            pltpu.VMEM((tz, d), BF16),
            pltpu.VMEM((ez, d), BF16),
            pltpu.VMEM((d, hd), BF16),
            pltpu.VMEM((d, 2 * hd), BF16),
            pltpu.VMEM((hd, d), BF16),
            pltpu.VMEM((table_rows, d), BF16),
            pltpu.VMEM((nz, 2, ez, hd), BF16),
            pltpu.VMEM((tz, hd + 128), F32),
            pltpu.VMEM((tg, hd + 128), F32),
            pltpu.VMEM((nv, ty, width), F32),
            pltpu.VMEM((nv, ty, width), F32),
            pltpu.VMEM((pieces, ty, 128), F32),
            pltpu.VMEM((nz, ng, ny, ty, d), BF16),
            pltpu.VMEM((table_rows, target), F32),
            pltpu.VMEM((nz // step_blocks, 8, step_blocks * tz), F32),
            pltpu.VMEM((nx * NC, 2 * stat_rows, 128), F32),
            pltpu.VMEM((ny, 2 * stat_rows, 128), F32),
            pltpu.VMEM((nz, 2 * stat_rows, 128), F32),
            dma((7,)),
            dma((2,)),
            dma((2, half, 2)),
            dma((2, half, 2)),
            dma((2,)),
            dma((nv,)),
            dma((nv,)),
            dma((pieces,)),
            dma((pieces,)),
            dma((3, most)),
            dma((3, most)),
            dma((3, most)),
            dma((3, most)),
            dma((2, half, 2)),
            dma((2, half, 2)),
            dma((2, most)),
            dma((2, most)),
            dma((3, most)),
            dma((3, most)),
            dma((3, max(most, nx * NC))),
            dma((3, max(most, nx * NC))),
        ],
        compiler_params=pltpu.CompilerParams(
            collective_id=0, has_side_effects=True, vmem_limit_bytes=48 * 1024 * 1024
        ),
    )(
        decoder_states,
        encoder_states,
        ln_gains,
        labels.reshape(1, target),
        src_length,
        tgt_length,
        w_query,
        w_key,
        w_value,
        w_out,
        embedding,
    )
    block = 128
    grad_table = pl.pallas_call(
        grad_kernel,
        out_shape=jax.ShapeDtypeStruct((table_rows, d), BF16),
        grid=(table_rows // block,),
        in_specs=[
            pl.BlockSpec((1, target), lambda i: (0, 0)),
            pl.BlockSpec((1, target), lambda i: (0, 0)),
            pl.BlockSpec((block, target), lambda i: (i, 0)),
            pl.BlockSpec((target, d), lambda i: (0, 0)),
        ],
        out_specs=pl.BlockSpec((block, d), lambda i: (i, 0)),
        compiler_params=pltpu.CompilerParams(vmem_limit_bytes=32 * 1024 * 1024),
    )(lse, hit, logit, rows.reshape(target, d))
    return (loss.reshape(target), grad_table)


def solution(mesh):
    nv, nz, ng = mesh.shape["vocab"], mesh.shape["seq"], mesh.shape["grp"]
    cfg = (nv, nz, ng, NY, nv // (NY * NC))
    in_specs = (
        P("seq", None),
        P(("seq", "grp"), None),
        P(),
        P(None, "vocab"),
        P(None, "vocab"),
        P(None, "vocab"),
        P("vocab", None),
        P(("vocab", "seq", "grp"), None),
        P(),
        P(),
        P(),
    )
    out_specs = (P(), P(("vocab", "seq", "grp"), None))
    return jax.shard_map(
        functools.partial(body, cfg), mesh=mesh, in_specs=in_specs, out_specs=out_specs, check_vma=False
    )
```

time: 470 us -> 109 us (0.23)
  blocking collectives: 222 us -> 0 us
  waiting for transfers between devices: 192 us -> 0 us
  Pallas kernels: 0 us -> 93.7 us
  matrix products: 25.2 us -> 0 us
  between operations: 15.4 us -> 1.96 us
  other arithmetic: 8.79 us -> 0 us
  local copies, waits for them, and re-layouts: 5.75 us -> 12.5 us
    psum x1 -> x0, waiting for transfers between devices: 136 us -> none  [body(): attention = lax.psum(partial_out, 'vocab')]
    pallas_call x0 -> x2, Pallas kernels: none -> 93.7 us  [the longest x1 87.6 us: body(): pl.pallas_call(functools.partial(front_kernel, cfg), out_shape=(jax.Shape...]
    pmax x1 -> x0, blocking collectives: 76.4 us -> none  [body(): row_max = lax.pmax(local_top, ('vocab', 'seq', 'grp'))]
    all_gather x2 -> x0, blocking collectives: 72.7 us -> none  [the longest x1 40.7 us: body(): lax.all_gather(value_rows, ('seq', 'grp'), axis=0, tiled=True)]
    psum x1 -> x0, blocking collectives: 72.7 us -> none  [body(): lax.psum((jnp.sum(exp_logits, axis=1), local_pick), ('vocab', 'seq', 'grp'))]
    all_gather x1 -> x0, waiting for transfers between devices: 55.5 us -> none  [body(): gathered = lax.all_gather(final_rows, 'seq', axis=0, tiled=True)]
    dot_general x6 -> x0, matrix products: 25.2 us -> none  [the longest x1 9.47 us: body(): lax.dot_general(grad_logits, gathered, (((0,), (0,)), ((), ())), preferre...]
    unnamed x8 -> x21, local copies, waits for them, and re-layouts: 0.03 us -> 12.5 us
  transfers between devices with their start and end apart: 2 -> 0, of which waited for: 2 -> 0; matrix products, arithmetic and copies ran while one was open for 0% -> 0% of each run, Pallas kernels for 0% -> 0%
where the time goes in v1:
time: 109 us; the launch traced here: 108 us
  Pallas kernels  93.7 us (86%)
  local copies, waits for them, and re-layouts  12.5 us (11%)
  between operations  1.96 us (2%)
    pallas_call x1, Pallas kernels, body(): pl.pallas_call(functools.partial(front_kernel, cfg), out_shape=(jax.Shape...  87.6 us
    unnamed x21, local copies, waits for them, and re-layouts  12.5 us
    pallas_call x1, Pallas kernels, body(): pl.pallas_call(grad_kernel, out_shape=jax.ShapeDtypeStruct((table_rows, d...  6.12 us

profile of v1, /device:TPU:1, one launch (start us, length us, event | category | flops | bytes accessed | tf_op | source)
XLA Modules:
  0.0 108.1 jit_solution(15862387729351268933)
XLA Ops:
  1.9 0.0 copy-start.2
  1.9 1.0 copy-done.2
  3.0 0.0 copy-start.3
  3.0 1.0 copy-done.3
  4.0 0.0 copy-start.4
  4.0 1.0 copy-done.4
  5.1 0.0 copy-start.5
  5.1 1.0 copy-done.5
  6.1 0.0 copy-start.6
  6.1 1.0 copy-done.6
  7.1 0.0 copy-start.7
  7.1 1.0 copy-done.7
  8.2 0.0 copy-start.8
  8.2 0.7 copy-done.8
  8.9 0.0 copy-start.9
  8.9 0.7 copy-done.9
  9.6 87.6 %shard_map.122 = (f32[8,128]{1,0:T(8,128)S(1)}, f32[1,1024]{1,0:T(1,128)S(1)}, s32[1,1024]{1,0:T(1,128)S(1)}, f32[896,1024]{1,0:T(8,128)}, bf16[8,2,4,16,2048]{4,3,2,1,0:T(8,128)(2,1)}) custom-call(bf16[128,2048]{1,0:T(8,128)(2,1)S(1)} %copy-done.2, bf16[128,2048]{1,0:T(8,128)(2,1)S(1)} %copy-done.3, f32[2,2048]{1,0:T(2,128)S(1)} %copy-done.8, ...), custom_call_target="tpu_custom_call" | custom-call | tf_op jit(solution)/shard_map/pallas_call | solution.py:525
  97.1 0.0 copy-start
  97.2 2.2 %copy-done = bf16[8,2,4,16,2048]{4,3,2,1,0:T(8,128)(2,1)S(1)} copy-done((bf16[8,2,4,16,2048]{4,3,2,1,0:T(8,128)(2,1)S(1)}, bf16[8,2,4,16,2048]{4,3,2,1,0:T(8,128)(2,1)}, u32[]{:S(2)}) %copy-start) | copy-done | bytes 4194328
  99.3 0.0 copy-start.1
  99.3 2.0 %copy-done.1 = f32[896,1024]{1,0:T(8,128)S(1)} copy-done((f32[896,1024]{1,0:T(8,128)S(1)}, f32[896,1024]{1,0:T(8,128)}, u32[]{:S(2)}) %copy-start.1) | copy-done | bytes 3670040
  101.4 6.1 %shard_map.123 = bf16[896,2048]{1,0:T(8,128)(2,1)} custom-call(f32[1,1024]{1,0:T(1,128)S(1)} %get-tuple-element.8.lse, s32[1,1024]{1,0:T(1,128)S(1)} %get-tuple-element.9.hit, f32[896,1024]{1,0:T(8,128)S(1)} %copy-done.1, bf16[1024,2048]{1,0:T(8,128)(2,1)S(1)} %bitcast.3), custom_call_target="tpu_custom_call" | custom-call | tf_op jit(solution)/shard_map/pallas_call | solution.py:594
  107.5 0.6 copy.16
Async XLA Ops:
  1.9 1.0 copy-start.2
  3.0 1.0 copy-start.3
  4.0 1.0 copy-start.4
  5.1 1.0 copy-start.5
  6.1 1.0 copy-start.6
  7.1 1.0 copy-start.7
  8.2 0.7 copy-start.8
  8.9 0.7 copy-start.9
  97.1 2.2 %copy-start = (bf16[8,2,4,16,2048]{4,3,2,1,0:T(8,128)(2,1)S(1)}, bf16[8,2,4,16,2048]{4,3,2,1,0:T(8,128)(2,1)}, u32[]{:S(2)}) copy-start(bf16[8,2,4,16,2048]{4,3,2,1,0:T(8,128)(2,1)} %get-tuple-element.11) | copy-start | bytes 12582916
  99.3 2.0 %copy-start.1 = (f32[896,1024]{1,0:T(8,128)S(1)}, f32[896,1024]{1,0:T(8,128)}, u32[]{:S(2)}) copy-start(f32[896,1024]{1,0:T(8,128)} %get-tuple-element.10.logit) | copy-start | bytes 11010052

commit v2 on v1

--- a/solution.py
+++ b/solution.py
@@ -19,22 +19,22 @@
 
 def front_kernel(
     cfg,
+    src_len,
+    tgt_len,
     dec_in,
     enc_in,
-    gains,
-    labels,
-    src_len,
-    tgt_len,
+    gains_in,
+    labels_in,
     wq_in,
     wk_in,
     wv_in,
     wo_in,
     emb_in,
     loss_out,
-    lse_out,
-    hit_out,
-    logit_out,
-    rows_out,
+    grad,
+    rows,
+    gains,
+    labels,
     dec,
     enc,
     wq,
@@ -47,14 +47,12 @@
     part,
     summed,
     norm_stat,
-    rows,
     logit,
     local_stat,
     stat_x,
     stat_y,
     stat_z,
     load_sem,
-    store_sem,
     kv_send,
     kv_recv,
     ctx_sem,
@@ -83,7 +81,7 @@
     tg = tz // ng
     ty = tg // ny
     width = d // (nxl * NC)
-    wa, wb = width // 2, width // 4
+    wa, wb, wc = width // 4, width // 4, width // 2
     table_rows = emb.shape[0]
     nx = ng * nxl
     half = nz // 2
@@ -134,6 +132,8 @@
                 (wq_in, wq),
                 (wo_in, wo),
                 (emb_in, emb),
+                (gains_in, gains),
+                (labels_in, labels),
             )
         )
     ]
@@ -193,6 +193,7 @@
     ring_post(kv_view, 0, kv_send, kv_recv)
 
     loads[3].wait()
+    loads[7].wait()
     states = dec[...].astype(F32)
     centred = states - jnp.mean(states, axis=1, keepdims=True)
     variance = jnp.mean(centred * centred, axis=1, keepdims=True)
@@ -247,7 +248,7 @@
         return (
             (base + xl_ * wa, wa),
             (base + nxl * wa + xl_ * wb, wb),
-            (base + nxl * (wa + wb) + xl_ * wb, wb),
+            (base + nxl * (wa + wb) + xl_ * wc, wc),
         )
 
     loads[5].wait()
@@ -309,7 +310,7 @@
         return (
             pl.ds(base, nxl * wa),
             pl.ds(pl.multiple_of(base + nxl * wa, 128), nxl * wb),
-            pl.ds(pl.multiple_of(base + nxl * (wa + wb), 128), nxl * wb),
+            pl.ds(pl.multiple_of(base + nxl * (wa + wb), 128), nxl * wc),
         )
 
     def cols_piece(xl_):
@@ -354,9 +355,8 @@
     def c3(x_):
         return rows.at[:, x_ // nxl, :, :, cols_piece(x_ % nxl)[2]]
 
-    def a3(block, part_):
-        base = pl.multiple_of(c * (d // NC) + part_ * (nxl * wa // 2), 128)
-        return rows.at[block, :, :, :, pl.ds(base, nxl * wa // 2)]
+    def a3(z_):
+        return rows.at[z_, :, :, :, all_a]
 
     exchange(nx, x, a1, first_send.at[0], first_recv.at[0], at_x)
     exchange(nz, z, b1, first_send.at[1], first_recv.at[1], at_z)
@@ -381,8 +381,8 @@
 
     def c_block(c_):
         def view(x_):
-            base = pl.multiple_of(c_ * (d // NC) + nxl * (wa + wb) + (x_ % nxl) * wb, 128)
-            return rows.at[:, x_ // nxl, :, :, pl.ds(base, wb)]
+            base = pl.multiple_of(c_ * (d // NC) + nxl * (wa + wb) + (x_ % nxl) * wc, 128)
+            return rows.at[:, x_ // nxl, :, :, pl.ds(base, wc)]
 
         return view
 
@@ -392,7 +392,7 @@
     share_a, share_b, share_c = share(0, a_block), share(1, b_block), share(2, c_block)
 
     collect(ny, y, a2, second_recv.at[0])
-    ring_post(a3, 0, ring_send, ring_recv)
+    exchange(nz, z, a3, ring_send, ring_recv, at_z)
     share_a(z)
     collect(nx, x, b2, second_recv.at[1])
     exchange(ny, y, b3, third_send.at[0], third_recv.at[0], at_y)
@@ -400,23 +400,15 @@
     collect(ny, y, c2, second_recv.at[2])
     exchange(nx, x, c3, third_send.at[1], third_recv.at[1], at_x)
     share_c(x)
-    for t in range(1, half + 1):
-        ring_wait(a3, t, ring_recv)
-        if t < half:
-            ring_post(a3, t, ring_send, ring_recv)
-        for block in ring_blocks(t):
-            share_a(block)
-        if t == half - 1:
-            collect(ny, y, b3, third_recv.at[0], share_b)
-            collect(nx, x, c3, third_recv.at[1], share_c)
+    collect(ny, y, b3, third_recv.at[0], share_b)
+    collect(nz, z, a3, ring_recv, share_a)
+    collect(nx, x, c3, third_recv.at[1], share_c)
     for kind, count, view in ((0, nz, a_block), (1, ny, b_block), (2, nx, c_block)):
         for i in range(count):
             arrived(view(1 - c)(i), core_recv.at[kind, i])
 
-    rows_store = pltpu.make_async_copy(rows, rows_out, store_sem.at[0])
-    rows_store.start()
-
     loads[6].wait()
+    loads[8].wait()
     table_base = ((v * nz + z) * ng + g) * table_rows
     step_blocks = max(1, 256 // tz)
     step_rows = step_blocks * tz
@@ -435,8 +427,6 @@
 
     steps = nz // step_blocks
     lax.fori_loop(0, steps, logit_step, 0)
-    logit_store = pltpu.make_async_copy(logit, logit_out, store_sem.at[1])
-    logit_store.start()
 
     stat_rows = nz * tz // 128
     per_step = step_rows // 128
@@ -471,22 +461,26 @@
     live = place < tgt_len[0]
     loss_out[...] = jnp.where(live, lse - picked, 0.0)
     lse = jnp.where(live, lse, 1e30)
-    for r in range(stat_rows):
-        lse_out[0:1, r * 128 : (r + 1) * 128] = lse[r : r + 1, :]
+    lse = jnp.concatenate([lse[r : r + 1, :] for r in range(stat_rows)], axis=1)
     place = lax.broadcasted_iota(jnp.int32, labels.shape, 1)
-    hit_out[...] = jnp.where(place < tgt_len[0], labels[...] - table_base, -1)
+    hit = jnp.where(place < tgt_len[0], labels[...] - table_base, -1)
+
+    def grad_step(i, carry):
+        some = pl.ds(i * 128, 128)
+        token = i * 128 + lax.broadcasted_iota(jnp.int32, (128, nz * tz), 0)
+        grad[some, :] = (jnp.exp(logit[some, :] - lse) - jnp.where(token == hit, 1.0, 0.0)).astype(BF16)
+        return carry
+
+    lax.fori_loop(0, table_rows // 128, grad_step, 0)
 
     for copy in sent:
         copy.wait_send()
-    rows_store.wait()
-    logit_store.wait()
-
-
-def grad_kernel(lse, hit, logit, rows, out):
-    base = pl.program_id(0) * out.shape[0]
-    token = base + lax.broadcasted_iota(jnp.int32, logit.shape, 0)
-    grad = jnp.exp(logit[...] - lse[...]) - jnp.where(token == hit[...], 1.0, 0.0)
-    out[...] = jnp.dot(grad.astype(BF16), rows[...], preferred_element_type=F32).astype(BF16)
+
+
+def grad_kernel(grad, rows, out):
+    cols = pl.ds(pl.multiple_of(pl.program_id(0) * out.shape[1], 128), out.shape[1])
+    chunk = rows[:, :, :, :, cols].reshape(grad.shape[1], out.shape[1])
+    out[...] = jnp.dot(grad[...], chunk, preferred_element_type=F32).astype(BF16)
 
 
 def body(
@@ -522,18 +516,32 @@
     vmem = pl.BlockSpec(memory_space=pltpu.VMEM)
     smem = pl.BlockSpec(memory_space=pltpu.SMEM)
     dma = pltpu.SemaphoreType.DMA
-    loss, lse, hit, logit, rows = pl.pallas_call(
+    far = [
+        pltpu.with_memory_space_constraint(array, pltpu.HBM)
+        for array in (
+            decoder_states,
+            encoder_states,
+            ln_gains,
+            labels.reshape(1, target),
+            w_query,
+            w_key,
+            w_value,
+            w_out,
+            embedding,
+        )
+    ]
+    loss, grad, rows = pl.pallas_call(
         functools.partial(front_kernel, cfg),
         out_shape=(
             jax.ShapeDtypeStruct((stat_rows, 128), F32),
-            jax.ShapeDtypeStruct((1, target), F32),
-            jax.ShapeDtypeStruct((1, target), jnp.int32),
-            jax.ShapeDtypeStruct((table_rows, target), F32),
-            jax.ShapeDtypeStruct((nz, ng, ny, ty, d), BF16),
+            pltpu.VMEM((table_rows, target), BF16),
+            pltpu.VMEM((nz, ng, ny, ty, d), BF16),
         ),
-        in_specs=[hbm, hbm, vmem, vmem, smem, smem, hbm, hbm, hbm, hbm, hbm],
-        out_specs=(vmem, vmem, vmem, hbm, hbm),
+        in_specs=[smem, smem] + [hbm] * len(far),
+        out_specs=(vmem, vmem, vmem),
         scratch_shapes=[
+            pltpu.VMEM(ln_gains.shape, F32),
+            pltpu.VMEM((1, target), jnp.int32),
             pltpu.VMEM((tz, d), BF16),
             pltpu.VMEM((ez, d), BF16),
             pltpu.VMEM((d, hd), BF16),
@@ -546,14 +554,12 @@
             pltpu.VMEM((nv, ty, width), F32),
             pltpu.VMEM((nv, ty, width), F32),
             pltpu.VMEM((pieces, ty, 128), F32),
-            pltpu.VMEM((nz, ng, ny, ty, d), BF16),
             pltpu.VMEM((table_rows, target), F32),
             pltpu.VMEM((nz // step_blocks, 8, step_blocks * tz), F32),
             pltpu.VMEM((nx * NC, 2 * stat_rows, 128), F32),
             pltpu.VMEM((ny, 2 * stat_rows, 128), F32),
             pltpu.VMEM((nz, 2 * stat_rows, 128), F32),
-            dma((7,)),
-            dma((2,)),
+            dma((9,)),
             dma((2, half, 2)),
             dma((2, half, 2)),
             dma((2,)),
@@ -565,8 +571,8 @@
             dma((3, most)),
             dma((3, most)),
             dma((3, most)),
-            dma((2, half, 2)),
-            dma((2, half, 2)),
+            dma((nz,)),
+            dma((nz,)),
             dma((2, most)),
             dma((2, most)),
             dma((3, most)),
@@ -575,35 +581,18 @@
             dma((3, max(most, nx * NC))),
         ],
         compiler_params=pltpu.CompilerParams(
-            collective_id=0, has_side_effects=True, vmem_limit_bytes=48 * 1024 * 1024
+            collective_id=0, has_side_effects=True, vmem_limit_bytes=40 * 1024 * 1024
         ),
-    )(
-        decoder_states,
-        encoder_states,
-        ln_gains,
-        labels.reshape(1, target),
-        src_length,
-        tgt_length,
-        w_query,
-        w_key,
-        w_value,
-        w_out,
-        embedding,
-    )
-    block = 128
+    )(src_length, tgt_length, *far)
+    block = 512
     grad_table = pl.pallas_call(
         grad_kernel,
         out_shape=jax.ShapeDtypeStruct((table_rows, d), BF16),
-        grid=(table_rows // block,),
-        in_specs=[
-            pl.BlockSpec((1, target), lambda i: (0, 0)),
-            pl.BlockSpec((1, target), lambda i: (0, 0)),
-            pl.BlockSpec((block, target), lambda i: (i, 0)),
-            pl.BlockSpec((target, d), lambda i: (0, 0)),
-        ],
-        out_specs=pl.BlockSpec((block, d), lambda i: (i, 0)),
-        compiler_params=pltpu.CompilerParams(vmem_limit_bytes=32 * 1024 * 1024),
-    )(lse, hit, logit, rows.reshape(target, d))
+        grid=(d // block,),
+        in_specs=[vmem, vmem],
+        out_specs=pl.BlockSpec((table_rows, block), lambda i: (0, i)),
+        compiler_params=pltpu.CompilerParams(vmem_limit_bytes=24 * 1024 * 1024),
+    )(*(pltpu.with_memory_space_constraint(array, pltpu.VMEM) for array in (grad, rows)))
     return (loss.reshape(target), grad_table)
 
 

time: 109 us -> 93.5 us (0.86)
  local copies, waits for them, and re-layouts: 12.5 us -> 0.59 us
  Pallas kernels: 93.7 us -> 90.8 us
    unnamed x21 -> x1, local copies, waits for them, and re-layouts: 12.5 us -> 0.59 us
    pallas_call x1, Pallas kernels: 87.6 us -> 85.4 us  [body(): pl.pallas_call(functools.partial(front_kernel, cfg), out_shape=(jax.Shape...]
where the time goes in v2:
time: 93.5 us; the launch traced here: 93.4 us
  Pallas kernels  90.8 us (97%)
  between operations  1.93 us (2%)
    pallas_call x1, Pallas kernels, body(): pl.pallas_call(functools.partial(front_kernel, cfg), out_shape=(jax.Shape...  85.4 us
    pallas_call x1, Pallas kernels, body(): pl.pallas_call(grad_kernel, out_shape=jax.ShapeDtypeStruct((table_rows, d...  5.42 us

profile of v2, /device:TPU:1, one launch (start us, length us, event | category | flops | bytes accessed | tf_op | source)
XLA Modules:
  0.0 93.4 jit_solution(8884591547473252158)
XLA Ops:
  1.9 85.4 %shard_map.122 = (f32[8,128]{1,0:T(8,128)S(1)}, bf16[896,1024]{1,0:T(8,128)(2,1)S(1)}, bf16[8,2,4,16,2048]{4,3,2,1,0:T(8,128)(2,1)S(1)}) custom-call(s32[1]{0:T(128)S(6)} %copy.14.src_len, s32[1]{0:T(128)S(6)} %copy.15.tgt_len, bf16[128,2048]{1,0:T(8,128)(2,1)} %dec_in.1, bf16[128,2048]{1,0:T(8,128)(2,1)} %enc_in.1, f32[2,2048]{1,0:T(2,128)} %gains_in.1, ...), custom_call_target="tpu_custom_call" | custom-call | tf_op jit(solution)/shard_map/pallas_call | solution.py:533
  87.4 5.4 %shard_map.123 = bf16[896,2048]{1,0:T(8,128)(2,1)} custom-call(bf16[896,1024]{1,0:T(8,128)(2,1)S(1)} %get-tuple-element.6.grad, bf16[8,2,4,16,2048]{4,3,2,1,0:T(8,128)(2,1)S(1)} %get-tuple-element.7.rows), custom_call_target="tpu_custom_call" | custom-call | tf_op jit(solution)/shard_map/pallas_call | solution.py:588
  92.8 0.6 copy.16

commit v3 on v2

--- a/solution.py
+++ b/solution.py
@@ -31,8 +31,8 @@
     wo_in,
     emb_in,
     loss_out,
-    grad,
-    rows,
+    grad_out,
+    rows_out,
     gains,
     labels,
     dec,
@@ -47,31 +47,21 @@
     part,
     summed,
     norm_stat,
+    rows,
     logit,
+    grad,
     local_stat,
     stat_x,
     stat_y,
     stat_z,
     load_sem,
-    kv_send,
+    store_sem,
     kv_recv,
-    ctx_sem,
-    sum_send,
-    sum_recv,
-    norm_send,
-    norm_recv,
-    first_send,
-    first_recv,
-    second_send,
-    second_recv,
-    ring_send,
-    ring_recv,
-    third_send,
-    third_recv,
-    core_send,
-    core_recv,
-    stat_send,
-    stat_recv,
+    a_recv,
+    b_recv,
+    c_recv,
+    send_sem,
+    recv_sem,
 ):
     nv, nz, ng, ny, nxl = cfg
     d = dec.shape[1]
@@ -129,77 +119,56 @@
                 (wk_in, wkv.at[:, 0:hd]),
                 (wv_in, wkv.at[:, hd : 2 * hd]),
                 (dec_in, dec),
+                (gains_in, gains),
                 (wq_in, wq),
                 (wo_in, wo),
+                (labels_in, labels),
                 (emb_in, emb),
-                (gains_in, gains),
-                (labels_in, labels),
             )
         )
     ]
-    for load in loads:
+    for load in loads[:6]:
         load.start()
 
-    sent = []
-
-    def send(ref, dst, send_sem, recv_sem, device):
-        copy = pltpu.make_async_remote_copy(
-            src_ref=ref,
-            dst_ref=dst,
-            send_sem=send_sem,
-            recv_sem=recv_sem,
-            device_id=device,
-            device_id_type=MESH,
+    def remote(src, dst, out_sem, in_sem, device):
+        return pltpu.make_async_remote_copy(
+            src_ref=src, dst_ref=dst, send_sem=out_sem, recv_sem=in_sem, device_id=device, device_id_type=MESH
         )
-        copy.start()
-        sent.append(copy)
-
-    def arrived(ref, recv_sem):
-        pltpu.make_async_remote_copy(
-            src_ref=ref,
-            dst_ref=ref,
-            send_sem=load_sem.at[0],
-            recv_sem=recv_sem,
-            device_id=at_z((z + 1) % nz),
-            device_id_type=MESH,
-        ).wait_recv()
-
-    def ring_post(view, t, send_sems, recv_sems):
-        for way, step in ((0, 1), (1, nz - 1)):
-            block = (z + t * (nz - step)) % nz
-            for part_ in (0, 1) if t + 1 < half else (way,):
-                ref = view(block, part_)
-                send(ref, ref, send_sems.at[way, t, part_], recv_sems.at[way, t, part_], at_z((z + step) % nz))
-
-    def ring_wait(view, t, recv_sems):
-        for way, step in ((0, 1), (1, nz - 1)):
-            block = (z + t * (nz - step)) % nz
-            for part_ in (0, 1) if t < half else (way,):
-                arrived(view(block, part_), recv_sems.at[way, t - 1, part_])
-
-    def ring_blocks(t):
-        return [(z + nz - t) % nz, (z + t) % nz] if t < half else [(z + half) % nz]
-
-    for i in (0, 1, 2):
-        loads[i].wait()
+
+    def arrived(ref, in_sem):
+        remote(ref, ref, send_sem.at[0], in_sem, at_z((z + 1) % nz)).wait_recv()
+
+    def left(ref, out_sem):
+        remote(ref, ref, out_sem, recv_sem.at[0], at_z((z + 1) % nz)).wait_send()
+
+    for load in loads[:3]:
+        load.wait()
+    for load in loads[6:]:
+        load.start()
     own_kv = jnp.dot(enc[...], wkv[...], preferred_element_type=F32).astype(BF16)
     kv[z, 0] = own_kv[:, 0:hd]
     kv[z, 1] = own_kv[:, hd : 2 * hd]
-    pl.semaphore_wait(barrier, len(friends))
-
-    def kv_view(block, part_):
-        return kv.at[block, part_]
-
-    ring_post(kv_view, 0, kv_send, kv_recv)
 
     loads[3].wait()
-    loads[7].wait()
+    loads[4].wait()
     states = dec[...].astype(F32)
     centred = states - jnp.mean(states, axis=1, keepdims=True)
     variance = jnp.mean(centred * centred, axis=1, keepdims=True)
     normed = (centred * lax.rsqrt(variance + EPSILON) * gains[0:1, :]).astype(BF16)
-    loads[4].wait()
+    loads[5].wait()
     query = (jnp.dot(normed, wq[...], preferred_element_type=F32) * (1.0 / math.sqrt(hd))).astype(BF16)
+
+    pl.semaphore_wait(barrier, len(friends))
+
+    def kv_post(way, t, part_):
+        step = (1, nz - 1)[way]
+        ref = kv.at[(z + t * (nz - step)) % nz, part_]
+        remote(ref, ref, send_sem.at[0], kv_recv.at[way, t, part_], at_z((z + step) % nz)).start()
+
+    for part_ in (0, 1):
+        for way in (0, 1):
+            if half > 1 or part_ == way:
+                kv_post(way, 0, part_)
 
     source_count = src_len[0]
 
@@ -211,10 +180,13 @@
 
     scored = [scores_of(z)]
     for t in range(1, half + 1):
-        ring_wait(kv_view, t, kv_recv)
-        if t < half:
-            ring_post(kv_view, t, kv_send, kv_recv)
-        scored += [scores_of(block) for block in ring_blocks(t)]
+        for part_ in (0, 1):
+            for way in (0, 1):
+                if t < half or part_ == way:
+                    arrived(kv.at[(z + t * (nz - (1, nz - 1)[way])) % nz, part_], kv_recv.at[way, t - 1, part_])
+                if t + 1 < half or (t + 1 == half and part_ == way):
+                    kv_post(way, t, part_)
+        scored += [scores_of((z + o) % nz) for o in ((nz - t, t) if t < half else (half,))]
     top = functools.reduce(jnp.maximum, [s for _, _, s in scored])
     top = jnp.max(top, axis=1, keepdims=True)
     total = jnp.zeros((tz, ez), F32)
@@ -227,14 +199,14 @@
     low = lax.broadcasted_iota(jnp.int32, (tz, 128), 1) < 64
     ctx_own[:, 0:hd] = acc
     ctx_own[:, hd : hd + 128] = jnp.where(low, top, total)
-    send(
+    remote(
         ctx_own.at[pl.ds(pl.multiple_of((1 - g) * tg, tg), tg)],
         ctx_got,
-        ctx_sem.at[0],
-        ctx_sem.at[1],
+        send_sem.at[1],
+        recv_sem.at[1],
         {"vocab": v, "seq": z, "grp": 1 - g},
-    )
-    arrived(ctx_got, ctx_sem.at[1])
+    ).start()
+    arrived(ctx_got, recv_sem.at[1])
     mine = ctx_own[pl.ds(pl.multiple_of(g * tg, tg), tg), :]
     other = ctx_got[...]
     top0, top1 = mine[:, hd : hd + 1], other[:, hd : hd + 1]
@@ -251,7 +223,7 @@
             (base + nxl * (wa + wb) + xl_ * wc, wc),
         )
 
-    loads[5].wait()
+    loads[6].wait()
     projected = jnp.dot(context, wo[...], preferred_element_type=F32)
     for xl_ in range(nxl):
         for y_ in range(ny):
@@ -264,16 +236,15 @@
                     at += size
     for o in range(1, nv):
         to = (v + o) % nv
-        send(part.at[to], summed.at[v], sum_send.at[o], sum_recv.at[v], at_v(to))
+        remote(part.at[to], summed.at[v], send_sem.at[2], recv_sem.at[2], at_v(to)).start()
     own_cols = [(pl.multiple_of(start, 128), size) for start, size in columns_of(xl, c)]
     own_row = pl.multiple_of(g * tg + y * ty, ty)
     hidden = part[v] + jnp.concatenate(
         [dec[pl.ds(own_row, ty), pl.ds(start, size)].astype(F32) for start, size in own_cols], axis=1
     )
+    arrived(summed.at[0 : nv - 1], recv_sem.at[2])
     for o in range(1, nv):
-        frm = (v + o) % nv
-        arrived(summed.at[frm], sum_recv.at[frm])
-        hidden = hidden + summed[frm]
+        hidden = hidden + summed[(v + o) % nv]
 
     piece = xl * NC + c
     pieces = nxl * NC
@@ -283,16 +254,14 @@
     norm_stat[piece] = jnp.where(low, own_mean, own_square)
     for o in range(1, pieces):
         to = (piece + o) % pieces
-        send(
+        remote(
             norm_stat.at[piece],
             norm_stat.at[piece],
-            norm_send.at[o],
-            norm_recv.at[piece],
+            send_sem.at[3],
+            recv_sem.at[3],
             at_v(vocab_of(to // NC, y, to % NC)),
-        )
-    for o in range(1, pieces):
-        frm = (piece + o) % pieces
-        arrived(norm_stat.at[frm], norm_recv.at[frm])
+        ).start()
+    arrived(norm_stat.at[0 : pieces - 1], recv_sem.at[3])
     means = [norm_stat[i, :, 0:1] for i in range(pieces)]
     squares = [norm_stat[i, :, 64:65] for i in range(pieces)]
     mean = sum(means) * (1.0 / pieces)
@@ -319,17 +288,10 @@
     own_a, own_b, own_c = cols_piece(xl)
     all_a, all_b, all_c = cols_all(c)
 
-    def exchange(n, me, ref_of, send_sems, recv_sems, device_of):
+    def exchange(n, me, ref_of, out_sem, in_sem, device_of):
+        ref = ref_of(me)
         for o in range(1, n):
-            ref = ref_of(me)
-            send(ref, ref, send_sems.at[o], recv_sems.at[me], device_of((me + o) % n))
-
-    def collect(n, me, ref_of, recv_sems, then=None):
-        for o in range(1, n):
-            frm = (me + o) % n
-            arrived(ref_of(frm), recv_sems.at[frm])
-            if then is not None:
-                then(frm)
+            remote(ref, ref, out_sem, in_sem, device_of((me + o) % n)).start()
 
     def a1(x_):
         return rows.at[z, x_ // nxl, y, :, cols_piece(x_ % nxl)[0]]
@@ -358,65 +320,102 @@
     def a3(z_):
         return rows.at[z_, :, :, :, all_a]
 
-    exchange(nx, x, a1, first_send.at[0], first_recv.at[0], at_x)
-    exchange(nz, z, b1, first_send.at[1], first_recv.at[1], at_z)
-    exchange(nz, z, c1, first_send.at[2], first_recv.at[2], at_z)
-    collect(nx, x, a1, first_recv.at[0])
-    exchange(ny, y, a2, second_send.at[0], second_recv.at[0], at_y)
-    collect(nz, z, b1, first_recv.at[1])
-    exchange(nx, x, b2, second_send.at[1], second_recv.at[1], at_x)
-    collect(nz, z, c1, first_recv.at[2])
-    exchange(ny, y, c2, second_send.at[2], second_recv.at[2], at_y)
+    all_a1 = rows.at[0, 0, 0 : nx - 1, :, 0:wa]
+    all_b1 = rows.at[0 : nz - 1, 0, 0, :, 0:wb]
+    all_c1 = rows.at[0 : nz - 1, 0, 0, :, 0:wc]
+    all_a2 = rows.at[0, :, 0 : ny - 1, :, 0 : nxl * wa]
+    all_b2 = rows.at[:, 0, 0 : nx - 1, :, 0:wb]
+    all_c2 = rows.at[:, 0, 0 : ny - 1, :, 0:wc]
+    all_a3 = rows.at[0 : nz - 1, :, :, :, 0 : nxl * wa]
+    all_b3 = rows.at[:, :, 0 : ny - 1, :, 0 : nxl * wb]
+    all_c3 = rows.at[:, 0, :, :, 0 : (nx - 1) * wc]
+
+    exchange(nx, x, a1, send_sem.at[4], recv_sem.at[4], at_x)
+    exchange(nz, z, c1, send_sem.at[6], recv_sem.at[6], at_z)
+    exchange(nz, z, b1, send_sem.at[5], recv_sem.at[5], at_z)
+    arrived(all_a1, recv_sem.at[4])
+    exchange(ny, y, a2, send_sem.at[7], recv_sem.at[7], at_y)
+    arrived(all_c1, recv_sem.at[6])
+    exchange(ny, y, c2, send_sem.at[9], recv_sem.at[9], at_y)
+    arrived(all_b1, recv_sem.at[5])
+    exchange(nx, x, b2, send_sem.at[8], recv_sem.at[8], at_x)
 
     sibling = at_x(x, 1 - c)
 
-    def to_core(kind, i, ref):
-        send(ref, ref, core_send.at[kind, i], core_recv.at[kind, i], sibling)
-
-    def a_block(c_):
-        return lambda z_: rows.at[z_, :, :, :, cols_all(c_)[0]]
-
-    def b_block(c_):
-        return lambda y_: rows.at[:, :, y_, :, cols_all(c_)[1]]
-
-    def c_block(c_):
-        def view(x_):
-            base = pl.multiple_of(c_ * (d // NC) + nxl * (wa + wb) + (x_ % nxl) * wc, 128)
-            return rows.at[:, x_ // nxl, :, :, pl.ds(base, wc)]
-
-        return view
-
-    def share(kind, view):
-        return lambda i: to_core(kind, i, view(c)(i))
-
-    share_a, share_b, share_c = share(0, a_block), share(1, b_block), share(2, c_block)
-
-    collect(ny, y, a2, second_recv.at[0])
-    exchange(nz, z, a3, ring_send, ring_recv, at_z)
-    share_a(z)
-    collect(nx, x, b2, second_recv.at[1])
-    exchange(ny, y, b3, third_send.at[0], third_recv.at[0], at_y)
-    share_b(y)
-    collect(ny, y, c2, second_recv.at[2])
-    exchange(nx, x, c3, third_send.at[1], third_recv.at[1], at_x)
-    share_c(x)
-    collect(ny, y, b3, third_recv.at[0], share_b)
-    collect(nz, z, a3, ring_recv, share_a)
-    collect(nx, x, c3, third_recv.at[1], share_c)
-    for kind, count, view in ((0, nz, a_block), (1, ny, b_block), (2, nx, c_block)):
-        for i in range(count):
-            arrived(view(1 - c)(i), core_recv.at[kind, i])
-
-    loads[6].wait()
+    def a_block(z_):
+        return rows.at[z_, :, :, :, all_a]
+
+    def b_block(y_):
+        return rows.at[:, :, y_, :, all_b]
+
+    def c_block(x_):
+        base = pl.multiple_of(c * (d // NC) + nxl * (wa + wb) + (x_ % nxl) * wc, 128)
+        return rows.at[:, x_ // nxl, :, :, pl.ds(base, wc)]
+
+    def share(kind, ref):
+        remote(ref, ref, send_sem.at[13 + kind], recv_sem.at[10 + kind], sibling).start()
+
+    arrived(all_a2, recv_sem.at[7])
+    ref = a3(z)
+    for o in range(1, nz):
+        remote(ref, ref, send_sem.at[10], a_recv.at[z], at_z((z + o) % nz)).start()
+    share(0, a_block(z))
+    arrived(all_c2, recv_sem.at[9])
+    ref = c3(x)
+    for o in range(1, nx):
+        remote(ref, ref, send_sem.at[12], c_recv.at[x], at_x((x + o) % nx)).start()
+    share(2, c_block(x))
+    arrived(all_b2, recv_sem.at[8])
+    ref = b3(y)
+    for o in range(1, ny):
+        remote(ref, ref, send_sem.at[11], b_recv.at[y], at_y((y + o) % ny)).start()
+    share(1, b_block(y))
+    for o in range(1, ny):
+        frm = (y + o) % ny
+        arrived(b3(frm), b_recv.at[frm])
+        share(1, b_block(frm))
+    for o in range(1, nz):
+        frm = (z + o) % nz
+        arrived(a3(frm), a_recv.at[frm])
+        share(0, a_block(frm))
+    their_a, their_b, their_c = cols_all(1 - c)
+    arrived(rows.at[:, :, :, :, their_a], recv_sem.at[10])
+    arrived(rows.at[:, :, :, :, their_b], recv_sem.at[11])
+    loads[7].wait()
     loads[8].wait()
     table_base = ((v * nz + z) * ng + g) * table_rows
     step_blocks = max(1, 256 // tz)
     step_rows = step_blocks * tz
+    early = nxl * (wa + wb)
+
+    def logits_of(i, starts, size):
+        total_ = None
+        for start in starts:
+            chunk = rows[pl.ds(i * step_blocks, step_blocks), :, :, :, start : start + size].reshape(step_rows, size)
+            values = lax.dot_general(emb[:, start : start + size], chunk, NT, preferred_element_type=F32)
+            total_ = values if total_ is None else total_ + values
+        return total_
+
+    def lanes_of(i):
+        return pl.ds(pl.multiple_of(i * step_rows, 128), step_rows)
+
+    def early_step(i, carry):
+        logit[:, lanes_of(i)] = logits_of(i, range(0, d, d // NC), early)
+        return carry
+
+    steps = nz // step_blocks
+    for o in range(1, nx):
+        frm = (x + o) % nx
+        arrived(c3(frm), c_recv.at[frm])
+        share(2, c_block(frm))
+    lax.fori_loop(0, steps, early_step, 0)
+    arrived(rows.at[:, :, :, :, their_c], recv_sem.at[12])
+    rows_store = pltpu.make_async_copy(rows, rows_out, store_sem.at[0])
+    rows_store.start()
 
     def logit_step(i, carry):
-        chunk = rows[pl.ds(i * step_blocks, step_blocks)].reshape(step_rows, d)
-        lanes = pl.ds(pl.multiple_of(i * step_rows, 128), step_rows)
-        values = lax.dot_general(emb[...], chunk, NT, preferred_element_type=F32)
+        lanes = lanes_of(i)
+        values = logit[:, lanes] + logits_of(i, range(early, d, d // NC), d // NC - early)
         logit[:, lanes] = values
         top_ = jnp.max(values, axis=0, keepdims=True)
         total_ = jnp.sum(jnp.exp(values - top_), axis=0, keepdims=True)
@@ -425,9 +424,7 @@
         local_stat[i, 1:2, :] = jnp.sum(jnp.where(token == labels[:, lanes], values, 0.0), axis=0, keepdims=True)
         return carry
 
-    steps = nz // step_blocks
     lax.fori_loop(0, steps, logit_step, 0)
-
     stat_rows = nz * tz // 128
     per_step = step_rows // 128
     nxc = nx * NC
@@ -445,8 +442,8 @@
         return top_ + jnp.log(total_), sum(ref[i, stat_rows : 2 * stat_rows] for i in range(n))
 
     def stat_round(ref, n, me, k, device_of):
-        exchange(n, me, lambda i: ref.at[i], stat_send.at[k], stat_recv.at[k], device_of)
-        collect(n, me, lambda i: ref.at[i], stat_recv.at[k])
+        exchange(n, me, lambda i: ref.at[i], send_sem.at[16 + k], recv_sem.at[13 + k], device_of)
+        arrived(ref.at[0 : n - 1], recv_sem.at[13 + k])
         return merge(ref, n)
 
     lse, picked = stat_round(stat_x, nxc, xc, 0, lambda i: at_x(i // NC, i % NC))
@@ -473,8 +470,34 @@
 
     lax.fori_loop(0, table_rows // 128, grad_step, 0)
 
-    for copy in sent:
-        copy.wait_send()
+    grad_store = pltpu.make_async_copy(grad, grad_out, store_sem.at[1])
+    grad_store.start()
+    for i, ref in enumerate(
+        (
+            kv.at[0 : nz - 1],
+            ctx_got,
+            part.at[0 : nv - 1],
+            norm_stat.at[0 : pieces - 1],
+            all_a1,
+            all_b1,
+            all_c1,
+            all_a2,
+            all_b2,
+            all_c2,
+            all_a3,
+            all_b3,
+            all_c3,
+            rows.at[:, :, :, :, all_a],
+            rows.at[:, :, :, :, all_b],
+            rows.at[:, :, :, :, all_c],
+            stat_x.at[0 : nxc - 1],
+            stat_y.at[0 : ny - 1],
+            stat_z.at[0 : nz - 1],
+        )
+    ):
+        left(ref, send_sem.at[i])
+    rows_store.wait()
+    grad_store.wait()
 
 
 def grad_kernel(grad, rows, out):
@@ -511,7 +534,6 @@
     pieces = nxl * NC
     step_blocks = max(1, 256 // tz)
     stat_rows = target // 128
-    most = max(nz, nx, ny)
     hbm = pl.BlockSpec(memory_space=pl.ANY)
     vmem = pl.BlockSpec(memory_space=pltpu.VMEM)
     smem = pl.BlockSpec(memory_space=pltpu.SMEM)
@@ -538,7 +560,7 @@
             pltpu.VMEM((nz, ng, ny, ty, d), BF16),
         ),
         in_specs=[smem, smem] + [hbm] * len(far),
-        out_specs=(vmem, vmem, vmem),
+        out_specs=(vmem, hbm, hbm),
         scratch_shapes=[
             pltpu.VMEM(ln_gains.shape, F32),
             pltpu.VMEM((1, target), jnp.int32),
@@ -554,31 +576,21 @@
             pltpu.VMEM((nv, ty, width), F32),
             pltpu.VMEM((nv, ty, width), F32),
             pltpu.VMEM((pieces, ty, 128), F32),
+            pltpu.VMEM((nz, ng, ny, ty, d), BF16),
             pltpu.VMEM((table_rows, target), F32),
+            pltpu.VMEM((table_rows, target), BF16),
             pltpu.VMEM((nz // step_blocks, 8, step_blocks * tz), F32),
             pltpu.VMEM((nx * NC, 2 * stat_rows, 128), F32),
             pltpu.VMEM((ny, 2 * stat_rows, 128), F32),
             pltpu.VMEM((nz, 2 * stat_rows, 128), F32),
             dma((9,)),
+            dma((2,)),
             dma((2, half, 2)),
-            dma((2, half, 2)),
-            dma((2,)),
-            dma((nv,)),
-            dma((nv,)),
-            dma((pieces,)),
-            dma((pieces,)),
-            dma((3, most)),
-            dma((3, most)),
-            dma((3, most)),
-            dma((3, most)),
             dma((nz,)),
-            dma((nz,)),
-            dma((2, most)),
-            dma((2, most)),
-            dma((3, most)),
-            dma((3, most)),
-            dma((3, max(most, nx * NC))),
-            dma((3, max(most, nx * NC))),
+            dma((ny,)),
+            dma((nx,)),
+            dma((19,)),
+            dma((16,)),
         ],
         compiler_params=pltpu.CompilerParams(
             collective_id=0, has_side_effects=True, vmem_limit_bytes=40 * 1024 * 1024

time: 93.5 us -> 89 us (0.952)
  Pallas kernels: 90.8 us -> 86.4 us
    pallas_call x1, Pallas kernels: 85.4 us -> 81 us  [body(): pl.pallas_call(functools.partial(front_kernel, cfg), out_shape=(jax.Shape...]
where the time goes in v3:
time: 89 us; the launch traced here: 88.9 us
  Pallas kernels  86.4 us (97%)
  between operations  1.93 us (2%)
    pallas_call x1, Pallas kernels, body(): pl.pallas_call(functools.partial(front_kernel, cfg), out_shape=(jax.Shape...  81 us
    pallas_call x1, Pallas kernels, body(): pl.pallas_call(grad_kernel, out_shape=jax.ShapeDtypeStruct((table_rows, d...  5.42 us

profile of v3, /device:TPU:1, one launch (start us, length us, event | category | flops | bytes accessed | tf_op | source)
XLA Modules:
  0.0 88.9 jit_solution(11091834091826520536)
XLA Ops:
  1.9 81.0 %shard_map.122 = (f32[8,128]{1,0:T(8,128)S(1)}, bf16[896,1024]{1,0:T(8,128)(2,1)S(1)}, bf16[8,2,4,16,2048]{4,3,2,1,0:T(8,128)(2,1)S(1)}) custom-call(s32[1]{0:T(128)S(6)} %copy.14.src_len, s32[1]{0:T(128)S(6)} %copy.15.tgt_len, bf16[128,2048]{1,0:T(8,128)(2,1)} %dec_in.1, bf16[128,2048]{1,0:T(8,128)(2,1)} %enc_in.1, f32[2,2048]{1,0:T(2,128)} %gains_in.1, ...), custom_call_target="tpu_custom_call" | custom-call | tf_op jit(solution)/shard_map/pallas_call | solution.py:555
  82.9 5.4 %shard_map.123 = bf16[896,2048]{1,0:T(8,128)(2,1)} custom-call(bf16[896,1024]{1,0:T(8,128)(2,1)S(1)} %get-tuple-element.6.grad, bf16[8,2,4,16,2048]{4,3,2,1,0:T(8,128)(2,1)S(1)} %get-tuple-element.7.rows), custom_call_target="tpu_custom_call" | custom-call | tf_op jit(solution)/shard_map/pallas_call | solution.py:600
  88.3 0.6 copy.16

commit v4 on v3

--- a/solution.py
+++ b/solution.py
@@ -102,12 +102,7 @@
     barrier = pltpu.get_barrier_semaphore()
     friends = [at_v((v + o) % nv) for o in range(1, nv)]
     friends += [at_z((z + o) % nz) for o in range(1, nz)]
-    friends += [
-        {"vocab": vocab_of(xl_, y, c_), "seq": z, "grp": (g + o) % ng}
-        for o in range(1, ng)
-        for xl_ in range(nxl)
-        for c_ in range(NC)
-    ]
+    friends += [{"vocab": v_, "seq": z, "grp": (g + o) % ng} for o in range(1, ng) for v_ in range(nv)]
     for friend in friends:
         pl.semaphore_signal(barrier, inc=1, device_id=friend, device_id_type=MESH)
 
@@ -149,6 +144,18 @@
     kv[z, 0] = own_kv[:, 0:hd]
     kv[z, 1] = own_kv[:, hd : 2 * hd]
 
+    pl.semaphore_wait(barrier, len(friends))
+
+    def kv_post(way, t, part_):
+        step = (1, nz - 1)[way]
+        ref = kv.at[(z + t * (nz - step)) % nz, part_]
+        remote(ref, ref, send_sem.at[0], kv_recv.at[way, t, part_], at_z((z + step) % nz)).start()
+
+    for part_ in (0, 1):
+        for way in (0, 1):
+            if half > 1 or part_ == way:
+                kv_post(way, 0, part_)
+
     loads[3].wait()
     loads[4].wait()
     states = dec[...].astype(F32)
@@ -157,18 +164,6 @@
     normed = (centred * lax.rsqrt(variance + EPSILON) * gains[0:1, :]).astype(BF16)
     loads[5].wait()
     query = (jnp.dot(normed, wq[...], preferred_element_type=F32) * (1.0 / math.sqrt(hd))).astype(BF16)
-
-    pl.semaphore_wait(barrier, len(friends))
-
-    def kv_post(way, t, part_):
-        step = (1, nz - 1)[way]
-        ref = kv.at[(z + t * (nz - step)) % nz, part_]
-        remote(ref, ref, send_sem.at[0], kv_recv.at[way, t, part_], at_z((z + step) % nz)).start()
-
-    for part_ in (0, 1):
-        for way in (0, 1):
-            if half > 1 or part_ == way:
-                kv_post(way, 0, part_)
 
     source_count = src_len[0]
 
@@ -224,7 +219,7 @@
         )
 
     loads[6].wait()
-    projected = jnp.dot(context, wo[...], preferred_element_type=F32)
+    projected = jnp.dot(context, wo[...], preferred_element_type=F32).astype(BF16)
     for xl_ in range(nxl):
         for y_ in range(ny):
             for c_ in range(NC):
@@ -239,12 +234,12 @@
         remote(part.at[to], summed.at[v], send_sem.at[2], recv_sem.at[2], at_v(to)).start()
     own_cols = [(pl.multiple_of(start, 128), size) for start, size in columns_of(xl, c)]
     own_row = pl.multiple_of(g * tg + y * ty, ty)
-    hidden = part[v] + jnp.concatenate(
+    hidden = part[v].astype(F32) + jnp.concatenate(
         [dec[pl.ds(own_row, ty), pl.ds(start, size)].astype(F32) for start, size in own_cols], axis=1
     )
     arrived(summed.at[0 : nv - 1], recv_sem.at[2])
     for o in range(1, nv):
-        hidden = hidden + summed[(v + o) % nv]
+        hidden = hidden + summed[(v + o) % nv].astype(F32)
 
     piece = xl * NC + c
     pieces = nxl * NC
@@ -285,7 +280,7 @@
     def cols_piece(xl_):
         return [pl.ds(pl.multiple_of(start, 128), size) for start, size in columns_of(xl_, c)]
 
-    own_a, own_b, own_c = cols_piece(xl)
+    _, own_b, own_c = cols_piece(xl)
     all_a, all_b, all_c = cols_all(c)
 
     def exchange(n, me, ref_of, out_sem, in_sem, device_of):
@@ -293,8 +288,22 @@
         for o in range(1, n):
             remote(ref, ref, out_sem, in_sem, device_of((me + o) % n)).start()
 
-    def a1(x_):
-        return rows.at[z, x_ // nxl, y, :, cols_piece(x_ % nxl)[0]]
+    swap = c
+
+    def pick(here, there):
+        return here + swap * (there - here)
+
+    def place_b(i):
+        return pick(x, i), pick(i, y)
+
+    def place_c(i):
+        return pick(i, x), pick(y, i)
+
+    def at_xy(xy):
+        return {"vocab": vocab_of(xy[0] % nxl, xy[1], c), "seq": z, "grp": xy[0] // nxl}
+
+    def a1(xy):
+        return rows.at[z, xy[0] // nxl, xy[1], :, cols_piece(xy[0] % nxl)[0]]
 
     def b1(z_):
         return rows.at[z_, g, y, :, own_b]
@@ -302,85 +311,88 @@
     def c1(z_):
         return rows.at[z_, g, y, :, own_c]
 
-    def a2(y_):
-        return rows.at[z, :, y_, :, all_a]
-
-    def b2(x_):
-        return rows.at[:, x_ // nxl, y, :, cols_piece(x_ % nxl)[1]]
-
-    def c2(y_):
-        return rows.at[:, g, y_, :, own_c]
-
-    def b3(y_):
-        return rows.at[:, :, y_, :, all_b]
-
-    def c3(x_):
-        return rows.at[:, x_ // nxl, :, :, cols_piece(x_ % nxl)[2]]
-
-    def a3(z_):
-        return rows.at[z_, :, :, :, all_a]
-
-    all_a1 = rows.at[0, 0, 0 : nx - 1, :, 0:wa]
+    def b2(xy):
+        return rows.at[:, xy[0] // nxl, xy[1], :, cols_piece(xy[0] % nxl)[1]]
+
+    def c2(xy):
+        return rows.at[:, xy[0] // nxl, xy[1], :, cols_piece(xy[0] % nxl)[2]]
+
+    def along_x(kind, x_):
+        return rows.at[:, x_ // nxl, :, :, cols_piece(x_ % nxl)[kind]]
+
+    def along_y(kind, y_):
+        return rows.at[:, :, y_, :, cols_all(c)[kind]]
+
+    all_a1 = rows.at[0, 0, 0, :, 0 : (nx * ny - 1) * wa]
     all_b1 = rows.at[0 : nz - 1, 0, 0, :, 0:wb]
     all_c1 = rows.at[0 : nz - 1, 0, 0, :, 0:wc]
-    all_a2 = rows.at[0, :, 0 : ny - 1, :, 0 : nxl * wa]
     all_b2 = rows.at[:, 0, 0 : nx - 1, :, 0:wb]
     all_c2 = rows.at[:, 0, 0 : ny - 1, :, 0:wc]
     all_a3 = rows.at[0 : nz - 1, :, :, :, 0 : nxl * wa]
     all_b3 = rows.at[:, :, 0 : ny - 1, :, 0 : nxl * wb]
     all_c3 = rows.at[:, 0, :, :, 0 : (nx - 1) * wc]
 
-    exchange(nx, x, a1, send_sem.at[4], recv_sem.at[4], at_x)
+    me_b, me_c = pick(y, x), pick(x, y)
+    ref = a1((x, y))
+    for o in range(1, nx * ny):
+        to = ((x + o) % nx, (y + o // nx) % ny)
+        remote(ref, ref, send_sem.at[4], recv_sem.at[4], at_xy(to)).start()
     exchange(nz, z, c1, send_sem.at[6], recv_sem.at[6], at_z)
     exchange(nz, z, b1, send_sem.at[5], recv_sem.at[5], at_z)
+
+    sibling = at_x(x, 1 - c)
+
+    def share(kind, ref):
+        remote(ref, ref, send_sem.at[12 + kind], recv_sem.at[7 + kind], sibling).start()
+
+    def last(view, kind, n, me, in_sems, device_of):
+        ref = view(kind, me)
+        for o in range(1, n):
+            remote(ref, ref, send_sem.at[9 + kind], in_sems.at[me], device_of((me + o) % n)).start()
+        share(kind, ref)
+
+    def last_in(view, kind, n, me, in_sems):
+        for o in range(1, n):
+            ref = view(kind, (me + o) % n)
+            arrived(ref, in_sems.at[(me + o) % n])
+            share(kind, ref)
+
+    def at_x_(i):
+        return at_x(i)
+
+    def slab(kind, z_):
+        return rows.at[z_, :, :, :, all_a]
+
     arrived(all_a1, recv_sem.at[4])
-    exchange(ny, y, a2, send_sem.at[7], recv_sem.at[7], at_y)
+    last(slab, 0, nz, z, a_recv, at_z)
     arrived(all_c1, recv_sem.at[6])
-    exchange(ny, y, c2, send_sem.at[9], recv_sem.at[9], at_y)
+    ref = c2((x, y))
+    for o in range(1, nx):
+        remote(ref, ref, send_sem.at[8], recv_sem.at[16], at_xy(place_b((me_b + o) % nx))).start()
     arrived(all_b1, recv_sem.at[5])
-    exchange(nx, x, b2, send_sem.at[8], recv_sem.at[8], at_x)
-
-    sibling = at_x(x, 1 - c)
-
-    def a_block(z_):
-        return rows.at[z_, :, :, :, all_a]
-
-    def b_block(y_):
-        return rows.at[:, :, y_, :, all_b]
-
-    def c_block(x_):
-        base = pl.multiple_of(c * (d // NC) + nxl * (wa + wb) + (x_ % nxl) * wc, 128)
-        return rows.at[:, x_ // nxl, :, :, pl.ds(base, wc)]
-
-    def share(kind, ref):
-        remote(ref, ref, send_sem.at[13 + kind], recv_sem.at[10 + kind], sibling).start()
-
-    arrived(all_a2, recv_sem.at[7])
-    ref = a3(z)
-    for o in range(1, nz):
-        remote(ref, ref, send_sem.at[10], a_recv.at[z], at_z((z + o) % nz)).start()
-    share(0, a_block(z))
-    arrived(all_c2, recv_sem.at[9])
-    ref = c3(x)
+    ref = b2((x, y))
     for o in range(1, nx):
-        remote(ref, ref, send_sem.at[12], c_recv.at[x], at_x((x + o) % nx)).start()
-    share(2, c_block(x))
-    arrived(all_b2, recv_sem.at[8])
-    ref = b3(y)
-    for o in range(1, ny):
-        remote(ref, ref, send_sem.at[11], b_recv.at[y], at_y((y + o) % ny)).start()
-    share(1, b_block(y))
-    for o in range(1, ny):
-        frm = (y + o) % ny
-        arrived(b3(frm), b_recv.at[frm])
-        share(1, b_block(frm))
-    for o in range(1, nz):
-        frm = (z + o) % nz
-        arrived(a3(frm), a_recv.at[frm])
-        share(0, a_block(frm))
+        remote(ref, ref, send_sem.at[7], recv_sem.at[15], at_xy(place_c((me_c + o) % nx))).start()
+    arrived(all_c2, recv_sem.at[16])
+
+    @pl.when(c == 0)
+    def _():
+        last(along_x, 2, nx, x, c_recv, at_x_)
+        arrived(all_b2, recv_sem.at[15])
+        last(along_y, 1, ny, y, b_recv, at_y)
+        last_in(along_y, 1, ny, y, b_recv)
+
+    @pl.when(c == 1)
+    def _():
+        last(along_y, 2, ny, y, c_recv, at_y)
+        arrived(all_b2, recv_sem.at[15])
+        last(along_x, 1, nx, x, b_recv, at_x_)
+        last_in(along_x, 1, nx, x, b_recv)
+
+    last_in(slab, 0, nz, z, a_recv)
     their_a, their_b, their_c = cols_all(1 - c)
-    arrived(rows.at[:, :, :, :, their_a], recv_sem.at[10])
-    arrived(rows.at[:, :, :, :, their_b], recv_sem.at[11])
+    arrived(rows.at[:, :, :, :, their_a], recv_sem.at[7])
+    arrived(rows.at[:, :, :, :, their_b], recv_sem.at[8])
     loads[7].wait()
     loads[8].wait()
     table_base = ((v * nz + z) * ng + g) * table_rows
@@ -404,12 +416,17 @@
         return carry
 
     steps = nz // step_blocks
-    for o in range(1, nx):
-        frm = (x + o) % nx
-        arrived(c3(frm), c_recv.at[frm])
-        share(2, c_block(frm))
+
+    @pl.when(c == 0)
+    def _():
+        last_in(along_x, 2, nx, x, c_recv)
+
+    @pl.when(c == 1)
+    def _():
+        last_in(along_y, 2, ny, y, c_recv)
+
     lax.fori_loop(0, steps, early_step, 0)
-    arrived(rows.at[:, :, :, :, their_c], recv_sem.at[12])
+    arrived(rows.at[:, :, :, :, their_c], recv_sem.at[9])
     rows_store = pltpu.make_async_copy(rows, rows_out, store_sem.at[0])
     rows_store.start()
 
@@ -442,8 +459,8 @@
         return top_ + jnp.log(total_), sum(ref[i, stat_rows : 2 * stat_rows] for i in range(n))
 
     def stat_round(ref, n, me, k, device_of):
-        exchange(n, me, lambda i: ref.at[i], send_sem.at[16 + k], recv_sem.at[13 + k], device_of)
-        arrived(ref.at[0 : n - 1], recv_sem.at[13 + k])
+        exchange(n, me, lambda i: ref.at[i], send_sem.at[15 + k], recv_sem.at[10 + k], device_of)
+        arrived(ref.at[0 : n - 1], recv_sem.at[10 + k])
         return merge(ref, n)
 
     lse, picked = stat_round(stat_x, nxc, xc, 0, lambda i: at_x(i // NC, i % NC))
@@ -481,7 +498,6 @@
             all_a1,
             all_b1,
             all_c1,
-            all_a2,
             all_b2,
             all_c2,
             all_a3,
@@ -500,7 +516,8 @@
     grad_store.wait()
 
 
-def grad_kernel(grad, rows, out):
+def grad_kernel(grad, rows, loss, out, loss_out):
+    loss_out[...] = loss[...]
     cols = pl.ds(pl.multiple_of(pl.program_id(0) * out.shape[1], 128), out.shape[1])
     chunk = rows[:, :, :, :, cols].reshape(grad.shape[1], out.shape[1])
     out[...] = jnp.dot(grad[...], chunk, preferred_element_type=F32).astype(BF16)
@@ -573,8 +590,8 @@
             pltpu.VMEM((nz, 2, ez, hd), BF16),
             pltpu.VMEM((tz, hd + 128), F32),
             pltpu.VMEM((tg, hd + 128), F32),
-            pltpu.VMEM((nv, ty, width), F32),
-            pltpu.VMEM((nv, ty, width), F32),
+            pltpu.VMEM((nv, ty, width), BF16),
+            pltpu.VMEM((nv, ty, width), BF16),
             pltpu.VMEM((pieces, ty, 128), F32),
             pltpu.VMEM((nz, ng, ny, ty, d), BF16),
             pltpu.VMEM((table_rows, target), F32),
@@ -589,22 +606,22 @@
             dma((nz,)),
             dma((ny,)),
             dma((nx,)),
-            dma((19,)),
-            dma((16,)),
+            dma((18,)),
+            dma((17,)),
         ],
         compiler_params=pltpu.CompilerParams(
             collective_id=0, has_side_effects=True, vmem_limit_bytes=40 * 1024 * 1024
         ),
     )(src_length, tgt_length, *far)
     block = 512
-    grad_table = pl.pallas_call(
+    grad_table, loss = pl.pallas_call(
         grad_kernel,
-        out_shape=jax.ShapeDtypeStruct((table_rows, d), BF16),
+        out_shape=(jax.ShapeDtypeStruct((table_rows, d), BF16), jax.ShapeDtypeStruct(loss.shape, F32)),
         grid=(d // block,),
-        in_specs=[vmem, vmem],
-        out_specs=pl.BlockSpec((table_rows, block), lambda i: (0, i)),
+        in_specs=[vmem, vmem, vmem],
+        out_specs=(pl.BlockSpec((table_rows, block), lambda i: (0, i)), pl.BlockSpec(loss.shape, lambda i: (0, 0))),
         compiler_params=pltpu.CompilerParams(vmem_limit_bytes=24 * 1024 * 1024),
-    )(*(pltpu.with_memory_space_constraint(array, pltpu.VMEM) for array in (grad, rows)))
+    )(*(pltpu.with_memory_space_constraint(array, pltpu.VMEM) for array in (grad, rows)), loss)
     return (loss.reshape(target), grad_table)
 
 

time: 89 us -> 85.3 us (0.958)
  Pallas kernels: 86.4 us -> 83.2 us
    pallas_call x1, Pallas kernels: 81 us -> 77.8 us  [body(): pl.pallas_call(functools.partial(front_kernel, cfg), out_shape=(jax.Shape...]
where the time goes in v4:
time: 85.3 us; the launch traced here: 85.2 us
  Pallas kernels  83.2 us (98%)
  between operations  1.93 us (2%)
    pallas_call x1, Pallas kernels, body(): pl.pallas_call(functools.partial(front_kernel, cfg), out_shape=(jax.Shape...  77.8 us
    pallas_call x1, Pallas kernels, body(): pl.pallas_call(grad_kernel, out_shape=(jax.ShapeDtypeStruct((table_rows,...  5.42 us

profile of v4, /device:TPU:1, one launch (start us, length us, event | category | flops | bytes accessed | tf_op | source)
XLA Modules:
  0.0 85.2 jit_solution(871315587825593044)
XLA Ops:
  1.9 77.8 %shard_map.122 = (f32[8,128]{1,0:T(8,128)S(1)}, bf16[896,1024]{1,0:T(8,128)(2,1)S(1)}, bf16[8,2,4,16,2048]{4,3,2,1,0:T(8,128)(2,1)S(1)}) custom-call(s32[1]{0:T(128)S(6)} %copy.13.src_len, s32[1]{0:T(128)S(6)} %copy.14.tgt_len, bf16[128,2048]{1,0:T(8,128)(2,1)} %dec_in.1, bf16[128,2048]{1,0:T(8,128)(2,1)} %enc_in.1, f32[2,2048]{1,0:T(2,128)} %gains_in.1, ...), custom_call_target="tpu_custom_call" | custom-call | tf_op jit(solution)/shard_map/pallas_call | solution.py:572
  79.8 5.4 %shard_map.123 = (bf16[896,2048]{1,0:T(8,128)(2,1)}, f32[8,128]{1,0:T(8,128)}) custom-call(bf16[896,1024]{1,0:T(8,128)(2,1)S(1)} %get-tuple-element.7.grad, bf16[8,2,4,16,2048]{4,3,2,1,0:T(8,128)(2,1)S(1)} %get-tuple-element.8.rows, f32[8,128]{1,0:T(8,128)S(1)} %get-tuple-element.9.loss), custom_call_target="tpu_custom_call" | custom-call | tf_op jit(solution)/shard_map/pallas_call | solution.py:617

commit v5 on v4

--- a/solution.py
+++ b/solution.py
@@ -103,8 +103,6 @@
     friends = [at_v((v + o) % nv) for o in range(1, nv)]
     friends += [at_z((z + o) % nz) for o in range(1, nz)]
     friends += [{"vocab": v_, "seq": z, "grp": (g + o) % ng} for o in range(1, ng) for v_ in range(nv)]
-    for friend in friends:
-        pl.semaphore_signal(barrier, inc=1, device_id=friend, device_id_type=MESH)
 
     loads = [
         pltpu.make_async_copy(src, dst, load_sem.at[i])
@@ -124,6 +122,8 @@
     ]
     for load in loads[:6]:
         load.start()
+    for friend in friends:
+        pl.semaphore_signal(barrier, inc=1, device_id=friend, device_id_type=MESH)
 
     def remote(src, dst, out_sem, in_sem, device):
         return pltpu.make_async_remote_copy(
@@ -153,8 +153,11 @@
 
     for part_ in (0, 1):
         for way in (0, 1):
-            if half > 1 or part_ == way:
+            if half > 1:
                 kv_post(way, 0, part_)
+    for part_ in (0, 1):
+        ref = kv.at[z, part_]
+        remote(ref, ref, send_sem.at[0], kv_recv.at[0, half - 1, part_], at_z((z + half) % nz)).start()
 
     loads[3].wait()
     loads[4].wait()
@@ -177,9 +180,9 @@
     for t in range(1, half + 1):
         for part_ in (0, 1):
             for way in (0, 1):
-                if t < half or part_ == way:
+                if t < half or way == 0:
                     arrived(kv.at[(z + t * (nz - (1, nz - 1)[way])) % nz, part_], kv_recv.at[way, t - 1, part_])
-                if t + 1 < half or (t + 1 == half and part_ == way):
+                if t + 1 < half:
                     kv_post(way, t, part_)
         scored += [scores_of((z + o) % nz) for o in ((nz - t, t) if t < half else (half,))]
     top = functools.reduce(jnp.maximum, [s for _, _, s in scored])
@@ -219,19 +222,24 @@
         )
 
     loads[6].wait()
-    projected = jnp.dot(context, wo[...], preferred_element_type=F32).astype(BF16)
-    for xl_ in range(nxl):
+    piece = xl * NC + c
+    pieces = nxl * NC
+    for op in range(pieces):
+        to_piece = (piece + op) % pieces
+        weights = jnp.concatenate(
+            [
+                wo[:, pl.ds(pl.multiple_of(start, 128), size)]
+                for start, size in columns_of(to_piece // NC, to_piece % NC)
+            ],
+            axis=1,
+        )
+        projected = jnp.dot(context, weights, preferred_element_type=F32).astype(BF16)
         for y_ in range(ny):
-            for c_ in range(NC):
-                at = 0
-                for start, size in columns_of(xl_, c_):
-                    part[vocab_of(xl_, y_, c_), :, at : at + size] = projected[
-                        y_ * ty : (y_ + 1) * ty, start : start + size
-                    ]
-                    at += size
-    for o in range(1, nv):
-        to = (v + o) % nv
-        remote(part.at[to], summed.at[v], send_sem.at[2], recv_sem.at[2], at_v(to)).start()
+            part[vocab_of(to_piece // NC, y_, to_piece % NC)] = projected[y_ * ty : (y_ + 1) * ty]
+        for oy in range(ny):
+            if op + oy > 0:
+                to = vocab_of(to_piece // NC, (y + oy) % ny, to_piece % NC)
+                remote(part.at[to], summed.at[v], send_sem.at[2], recv_sem.at[2], at_v(to)).start()
     own_cols = [(pl.multiple_of(start, 128), size) for start, size in columns_of(xl, c)]
     own_row = pl.multiple_of(g * tg + y * ty, ty)
     hidden = part[v].astype(F32) + jnp.concatenate(
@@ -241,8 +249,6 @@
     for o in range(1, nv):
         hidden = hidden + summed[(v + o) % nv].astype(F32)
 
-    piece = xl * NC + c
-    pieces = nxl * NC
     own_mean = jnp.mean(hidden, axis=1, keepdims=True)
     own_square = jnp.sum((hidden - own_mean) * (hidden - own_mean), axis=1, keepdims=True)
     low = lax.broadcasted_iota(jnp.int32, (ty, 128), 1) < 64
@@ -333,13 +339,13 @@
     all_c3 = rows.at[:, 0, :, :, 0 : (nx - 1) * wc]
 
     me_b, me_c = pick(y, x), pick(x, y)
+    exchange(nz, z, c1, send_sem.at[6], recv_sem.at[6], at_z)
+    exchange(nz, z, b1, send_sem.at[5], recv_sem.at[5], at_z)
+
     ref = a1((x, y))
     for o in range(1, nx * ny):
         to = ((x + o) % nx, (y + o // nx) % ny)
         remote(ref, ref, send_sem.at[4], recv_sem.at[4], at_xy(to)).start()
-    exchange(nz, z, c1, send_sem.at[6], recv_sem.at[6], at_z)
-    exchange(nz, z, b1, send_sem.at[5], recv_sem.at[5], at_z)
-
     sibling = at_x(x, 1 - c)
 
     def share(kind, ref):
@@ -458,8 +464,10 @@
         total_ = sum(jnp.exp(s - top_) for s in lses)
         return top_ + jnp.log(total_), sum(ref[i, stat_rows : 2 * stat_rows] for i in range(n))
 
-    def stat_round(ref, n, me, k, device_of):
+    def stat_round(ref, n, me, k, device_of, meanwhile=None):
         exchange(n, me, lambda i: ref.at[i], send_sem.at[15 + k], recv_sem.at[10 + k], device_of)
+        if meanwhile is not None:
+            meanwhile()
         arrived(ref.at[0 : n - 1], recv_sem.at[10 + k])
         return merge(ref, n)
 
@@ -469,7 +477,33 @@
     lse, picked = stat_round(stat_y, ny, y, 1, at_y)
     stat_z[z, 0:stat_rows] = lse
     stat_z[z, stat_rows : 2 * stat_rows] = picked
-    lse, picked = stat_round(stat_z, nz, z, 2, at_z)
+
+    def settle():
+        for i, ref in enumerate(
+            (
+                kv.at[0 : nz - 1],
+                ctx_got,
+                part.at[0 : nv - 1],
+                norm_stat.at[0 : pieces - 1],
+                all_a1,
+                all_b1,
+                all_c1,
+                all_b2,
+                all_c2,
+                all_a3,
+                all_b3,
+                all_c3,
+                rows.at[:, :, :, :, all_a],
+                rows.at[:, :, :, :, all_b],
+                rows.at[:, :, :, :, all_c],
+                stat_x.at[0 : nxc - 1],
+                stat_y.at[0 : ny - 1],
+            )
+        ):
+            left(ref, send_sem.at[i])
+        rows_store.wait()
+
+    lse, picked = stat_round(stat_z, nz, z, 2, at_z, settle)
 
     place = lax.broadcasted_iota(jnp.int32, lse.shape, 0) * 128 + lax.broadcasted_iota(jnp.int32, lse.shape, 1)
     live = place < tgt_len[0]
@@ -483,44 +517,29 @@
         some = pl.ds(i * 128, 128)
         token = i * 128 + lax.broadcasted_iota(jnp.int32, (128, nz * tz), 0)
         grad[some, :] = (jnp.exp(logit[some, :] - lse) - jnp.where(token == hit, 1.0, 0.0)).astype(BF16)
+        pltpu.make_async_copy(grad.at[some], grad_out.at[some], store_sem.at[1]).start()
         return carry
 
     lax.fori_loop(0, table_rows // 128, grad_step, 0)
 
-    grad_store = pltpu.make_async_copy(grad, grad_out, store_sem.at[1])
-    grad_store.start()
-    for i, ref in enumerate(
-        (
-            kv.at[0 : nz - 1],
-            ctx_got,
-            part.at[0 : nv - 1],
-            norm_stat.at[0 : pieces - 1],
-            all_a1,
-            all_b1,
-            all_c1,
-            all_b2,
-            all_c2,
-            all_a3,
-            all_b3,
-            all_c3,
-            rows.at[:, :, :, :, all_a],
-            rows.at[:, :, :, :, all_b],
-            rows.at[:, :, :, :, all_c],
-            stat_x.at[0 : nxc - 1],
-            stat_y.at[0 : ny - 1],
-            stat_z.at[0 : nz - 1],
-        )
-    ):
-        left(ref, send_sem.at[i])
-    rows_store.wait()
-    grad_store.wait()
-
-
-def grad_kernel(grad, rows, loss, out, loss_out):
+    left(stat_z.at[0 : nz - 1], send_sem.at[17])
+    pltpu.make_async_copy(grad, grad_out, store_sem.at[1]).wait()
+
+
+def grad_kernel(tgt_len, grad, rows, loss, out, loss_out):
     loss_out[...] = loss[...]
-    cols = pl.ds(pl.multiple_of(pl.program_id(0) * out.shape[1], 128), out.shape[1])
-    chunk = rows[:, :, :, :, cols].reshape(grad.shape[1], out.shape[1])
-    out[...] = jnp.dot(grad[...], chunk, preferred_element_type=F32).astype(BF16)
+    nz, block = rows.shape[0], out.shape[1]
+    tz = grad.shape[1] // nz
+    cols = pl.ds(pl.multiple_of(pl.program_id(0) * block, 128), block)
+    step = max(1, 256 // tz)
+    live = (tgt_len[0] + step * tz - 1) // (step * tz)
+    for n in range(1, nz // step + 1):
+
+        @pl.when(jnp.clip(live, 1, nz // step) == n)
+        def _():
+            count = n * step * tz
+            chunk = rows[0 : n * step, :, :, :, cols].reshape(count, block)
+            out[...] = jnp.dot(grad[:, 0:count], chunk, preferred_element_type=F32).astype(BF16)
 
 
 def body(
@@ -618,10 +637,10 @@
         grad_kernel,
         out_shape=(jax.ShapeDtypeStruct((table_rows, d), BF16), jax.ShapeDtypeStruct(loss.shape, F32)),
         grid=(d // block,),
-        in_specs=[vmem, vmem, vmem],
+        in_specs=[smem, vmem, vmem, vmem],
         out_specs=(pl.BlockSpec((table_rows, block), lambda i: (0, i)), pl.BlockSpec(loss.shape, lambda i: (0, 0))),
         compiler_params=pltpu.CompilerParams(vmem_limit_bytes=24 * 1024 * 1024),
-    )(*(pltpu.with_memory_space_constraint(array, pltpu.VMEM) for array in (grad, rows)), loss)
+    )(tgt_length, *(pltpu.with_memory_space_constraint(array, pltpu.VMEM) for array in (grad, rows)), loss)
     return (loss.reshape(target), grad_table)
 
 

time: 85.3 us -> 83.6 us (0.980)
  Pallas kernels: 83.2 us -> 81.5 us
    pallas_call x1, Pallas kernels: 77.8 us -> 75.9 us  [body(): pl.pallas_call(functools.partial(front_kernel, cfg), out_shape=(jax.Shape...]
where the time goes in v5:
time: 83.6 us; the launch traced here: 83.4 us
  Pallas kernels  81.5 us (97%)
  between operations  1.93 us (2%)
    pallas_call x1, Pallas kernels, body(): pl.pallas_call(functools.partial(front_kernel, cfg), out_shape=(jax.Shape...  75.9 us
    pallas_call x1, Pallas kernels, body(): pl.pallas_call(grad_kernel, out_shape=(jax.ShapeDtypeStruct((table_rows,...  5.57 us

profile of v5, /device:TPU:1, one launch (start us, length us, event | category | flops | bytes accessed | tf_op | source)
XLA Modules:
  0.0 83.4 jit_solution(14310691674044160011)
XLA Ops:
  1.9 75.9 %shard_map.122 = (f32[8,128]{1,0:T(8,128)S(1)}, bf16[896,1024]{1,0:T(8,128)(2,1)S(1)}, bf16[8,2,4,16,2048]{4,3,2,1,0:T(8,128)(2,1)S(1)}) custom-call(s32[1]{0:T(128)S(6)} %copy.13.src_len, s32[1]{0:T(128)S(6)} %copy.14.tgt_len, bf16[128,2048]{1,0:T(8,128)(2,1)} %dec_in.1, bf16[128,2048]{1,0:T(8,128)(2,1)} %enc_in.1, f32[2,2048]{1,0:T(2,128)} %gains_in.1, ...), custom_call_target="tpu_custom_call" | custom-call | tf_op jit(solution)/shard_map/pallas_call | solution.py:591
  77.9 5.6 %shard_map.123 = (bf16[896,2048]{1,0:T(8,128)(2,1)}, f32[8,128]{1,0:T(8,128)}) custom-call(s32[1]{0:T(128)S(6)} %copy.14.tgt_len, bf16[896,1024]{1,0:T(8,128)(2,1)S(1)} %get-tuple-element.7.grad, bf16[8,2,4,16,2048]{4,3,2,1,0:T(8,128)(2,1)S(1)} %get-tuple-element.8.rows, f32[8,128]{1,0:T(8,128)S(1)} %get-tuple-element.9.loss), custom_call_target="tpu_custom_call" | custom-call | tf_op jit(solution)/shard_map/pallas_call | solution.py:636

commit v6 on v5

--- a/solution.py
+++ b/solution.py
@@ -100,9 +100,12 @@
         return {"vocab": v_, "seq": z, "grp": g}
 
     barrier = pltpu.get_barrier_semaphore()
-    friends = [at_v((v + o) % nv) for o in range(1, nv)]
-    friends += [at_z((z + o) % nz) for o in range(1, nz)]
+    def far_first(n):
+        return sorted(range(1, n), key=lambda o: -min(o, n - o))
+
+    friends = [at_z((z + o) % nz) for o in far_first(nz)]
     friends += [{"vocab": v_, "seq": z, "grp": (g + o) % ng} for o in range(1, ng) for v_ in range(nv)]
+    friends += [at_v((v + o) % nv) for o in range(1, nv)]
 
     loads = [
         pltpu.make_async_copy(src, dst, load_sem.at[i])
@@ -224,7 +227,7 @@
     loads[6].wait()
     piece = xl * NC + c
     pieces = nxl * NC
-    for op in range(pieces):
+    for op in [pieces // 2, *(o for o in range(pieces - 1, -1, -1) if o != pieces // 2)]:
         to_piece = (piece + op) % pieces
         weights = jnp.concatenate(
             [
@@ -236,7 +239,7 @@
         projected = jnp.dot(context, weights, preferred_element_type=F32).astype(BF16)
         for y_ in range(ny):
             part[vocab_of(to_piece // NC, y_, to_piece % NC)] = projected[y_ * ty : (y_ + 1) * ty]
-        for oy in range(ny):
+        for oy in [*far_first(ny), 0]:
             if op + oy > 0:
                 to = vocab_of(to_piece // NC, (y + oy) % ny, to_piece % NC)
                 remote(part.at[to], summed.at[v], send_sem.at[2], recv_sem.at[2], at_v(to)).start()
@@ -291,7 +294,7 @@
 
     def exchange(n, me, ref_of, out_sem, in_sem, device_of):
         ref = ref_of(me)
-        for o in range(1, n):
+        for o in far_first(n):
             remote(ref, ref, out_sem, in_sem, device_of((me + o) % n)).start()
 
     swap = c
@@ -343,7 +346,8 @@
     exchange(nz, z, b1, send_sem.at[5], recv_sem.at[5], at_z)
 
     ref = a1((x, y))
-    for o in range(1, nx * ny):
+    hops = [(min(o % nx, nx - o % nx) + min(o // nx, ny - o // nx), o) for o in range(1, nx * ny)]
+    for _, o in sorted(hops, reverse=True):
         to = ((x + o) % nx, (y + o // nx) % ny)
         remote(ref, ref, send_sem.at[4], recv_sem.at[4], at_xy(to)).start()
     sibling = at_x(x, 1 - c)
@@ -353,18 +357,55 @@
 
     def last(view, kind, n, me, in_sems, device_of):
         ref = view(kind, me)
-        for o in range(1, n):
+        for o in far_first(n):
             remote(ref, ref, send_sem.at[9 + kind], in_sems.at[me], device_of((me + o) % n)).start()
         share(kind, ref)
 
     def last_in(view, kind, n, me, in_sems):
-        for o in range(1, n):
+        for o in reversed(far_first(n)):
             ref = view(kind, (me + o) % n)
             arrived(ref, in_sems.at[(me + o) % n])
             share(kind, ref)
 
     def at_x_(i):
         return at_x(i)
+
+    mid = nz // 2
+
+    def half_x(i, part_):
+        return rows.at[part_ * mid : (part_ + 1) * mid, i // nxl, :, :, cols_piece(i % nxl)[2]]
+
+    def half_y(i, part_):
+        return rows.at[part_ * mid : (part_ + 1) * mid, :, i, :, all_c]
+
+    def relay_send(view, block, part_, sem, to, device_of):
+        ref = view(block, part_)
+        remote(ref, ref, send_sem.at[11], c_recv.at[sem], device_of(to)).start()
+
+    def relay_get(view, block, part_, sem):
+        ref = view(block, part_)
+        arrived(ref, c_recv.at[sem])
+        share(2, ref)
+
+    def relay_start(view, me, device_of):
+        for first in (0, 1):
+            relay_send(view, me, first, first, (me + 1) % nx, device_of)
+            relay_send(view, me, 1 - first, 3 - first, (me + nx - 1) % nx, device_of)
+        for part_ in (0, 1):
+            share(2, view(me, part_))
+
+    def relay_pass(view, me, device_of):
+        down, up = (me + nx - 1) % nx, (me + 1) % nx
+        relay_get(view, down, 0, 0)
+        relay_send(view, down, 0, 4, up, device_of)
+        relay_get(view, up, 1, 3)
+        relay_send(view, up, 1, 5, down, device_of)
+
+    def relay_end(view, me):
+        relay_get(view, (me + nx - 1) % nx, 1, 1)
+        relay_get(view, (me + 1) % nx, 0, 2)
+        relay_get(view, (me + 2) % nx, 0, 4)
+        relay_get(view, (me + 2) % nx, 1, 5)
 
     def slab(kind, z_):
         return rows.at[z_, :, :, :, all_a]
@@ -373,26 +414,28 @@
     last(slab, 0, nz, z, a_recv, at_z)
     arrived(all_c1, recv_sem.at[6])
     ref = c2((x, y))
-    for o in range(1, nx):
+    for o in far_first(nx):
         remote(ref, ref, send_sem.at[8], recv_sem.at[16], at_xy(place_b((me_b + o) % nx))).start()
     arrived(all_b1, recv_sem.at[5])
     ref = b2((x, y))
-    for o in range(1, nx):
+    for o in far_first(nx):
         remote(ref, ref, send_sem.at[7], recv_sem.at[15], at_xy(place_c((me_c + o) % nx))).start()
     arrived(all_c2, recv_sem.at[16])
 
     @pl.when(c == 0)
     def _():
-        last(along_x, 2, nx, x, c_recv, at_x_)
+        relay_start(half_x, x, at_x_)
         arrived(all_b2, recv_sem.at[15])
         last(along_y, 1, ny, y, b_recv, at_y)
+        relay_pass(half_x, x, at_x_)
         last_in(along_y, 1, ny, y, b_recv)
 
     @pl.when(c == 1)
     def _():
-        last(along_y, 2, ny, y, c_recv, at_y)
+        relay_start(half_y, y, at_y)
         arrived(all_b2, recv_sem.at[15])
         last(along_x, 1, nx, x, b_recv, at_x_)
+        relay_pass(half_y, y, at_y)
         last_in(along_x, 1, nx, x, b_recv)
 
     last_in(slab, 0, nz, z, a_recv)
@@ -425,19 +468,19 @@
 
     @pl.when(c == 0)
     def _():
-        last_in(along_x, 2, nx, x, c_recv)
+        relay_end(half_x, x)
 
     @pl.when(c == 1)
     def _():
-        last_in(along_y, 2, ny, y, c_recv)
+        relay_end(half_y, y)
 
     lax.fori_loop(0, steps, early_step, 0)
     arrived(rows.at[:, :, :, :, their_c], recv_sem.at[9])
     rows_store = pltpu.make_async_copy(rows, rows_out, store_sem.at[0])
     rows_store.start()
 
-    def logit_step(i, carry):
-        lanes = lanes_of(i)
+    for i in range(steps):
+        lanes = pl.ds(i * step_rows, step_rows)
         values = logit[:, lanes] + logits_of(i, range(early, d, d // NC), d // NC - early)
         logit[:, lanes] = values
         top_ = jnp.max(values, axis=0, keepdims=True)
@@ -445,9 +488,7 @@
         token = table_base + lax.broadcasted_iota(jnp.int32, values.shape, 0)
         local_stat[i, 0:1, :] = top_ + jnp.log(total_)
         local_stat[i, 1:2, :] = jnp.sum(jnp.where(token == labels[:, lanes], values, 0.0), axis=0, keepdims=True)
-        return carry
-
-    lax.fori_loop(0, steps, logit_step, 0)
+
     stat_rows = nz * tz // 128
     per_step = step_rows // 128
     nxc = nx * NC
@@ -624,7 +665,7 @@
             dma((2, half, 2)),
             dma((nz,)),
             dma((ny,)),
-            dma((nx,)),
+            dma((6,)),
             dma((18,)),
             dma((17,)),
         ],

time: 83.6 us -> 81.5 us (0.975)
  Pallas kernels: 81.5 us -> 79.5 us
    pallas_call x1, Pallas kernels: 75.9 us -> 73.9 us  [body(): pl.pallas_call(functools.partial(front_kernel, cfg), out_shape=(jax.Shape...]
where the time goes in v6:
time: 81.5 us; the launch traced here: 81.4 us
  Pallas kernels  79.5 us (98%)
  between operations  1.93 us (2%)
    pallas_call x1, Pallas kernels, body(): pl.pallas_call(functools.partial(front_kernel, cfg), out_shape=(jax.Shape...  73.9 us
    pallas_call x1, Pallas kernels, body(): pl.pallas_call(grad_kernel, out_shape=(jax.ShapeDtypeStruct((table_rows,...  5.56 us

profile of v6, /device:TPU:1, one launch (start us, length us, event | category | flops | bytes accessed | tf_op | source)
XLA Modules:
  0.0 81.4 jit_solution(2278713975878822731)
XLA Ops:
  1.9 73.9 %shard_map.122 = (f32[8,128]{1,0:T(8,128)S(1)}, bf16[896,1024]{1,0:T(8,128)(2,1)S(1)}, bf16[8,2,4,16,2048]{4,3,2,1,0:T(8,128)(2,1)S(1)}) custom-call(s32[1]{0:T(128)S(6)} %copy.13.src_len, s32[1]{0:T(128)S(6)} %copy.14.tgt_len, bf16[128,2048]{1,0:T(8,128)(2,1)} %dec_in.1, bf16[128,2048]{1,0:T(8,128)(2,1)} %enc_in.1, f32[2,2048]{1,0:T(2,128)} %gains_in.1, ...), custom_call_target="tpu_custom_call" | custom-call | tf_op jit(solution)/shard_map/pallas_call | solution.py:632
  75.9 5.6 %shard_map.123 = (bf16[896,2048]{1,0:T(8,128)(2,1)}, f32[8,128]{1,0:T(8,128)}) custom-call(s32[1]{0:T(128)S(6)} %copy.14.tgt_len, bf16[896,1024]{1,0:T(8,128)(2,1)S(1)} %get-tuple-element.7.grad, bf16[8,2,4,16,2048]{4,3,2,1,0:T(8,128)(2,1)S(1)} %get-tuple-element.8.rows, f32[8,128]{1,0:T(8,128)S(1)} %get-tuple-element.9.loss), custom_call_target="tpu_custom_call" | custom-call | tf_op jit(solution)/shard_map/pallas_call | solution.py:677

commit v7 on v6

--- a/solution.py
+++ b/solution.py
@@ -499,25 +499,21 @@
                 r // per_step, k : k + 1, (r % per_step) * 128 : (r % per_step + 1) * 128
             ]
 
-    def merge(ref, n):
-        lses = [ref[i, 0:stat_rows] for i in range(n)]
-        top_ = functools.reduce(jnp.maximum, lses)
-        total_ = sum(jnp.exp(s - top_) for s in lses)
-        return top_ + jnp.log(total_), sum(ref[i, stat_rows : 2 * stat_rows] for i in range(n))
-
-    def stat_round(ref, n, me, k, device_of, meanwhile=None):
-        exchange(n, me, lambda i: ref.at[i], send_sem.at[15 + k], recv_sem.at[10 + k], device_of)
-        if meanwhile is not None:
-            meanwhile()
-        arrived(ref.at[0 : n - 1], recv_sem.at[10 + k])
-        return merge(ref, n)
-
-    lse, picked = stat_round(stat_x, nxc, xc, 0, lambda i: at_x(i // NC, i % NC))
-    stat_y[y, 0:stat_rows] = lse
-    stat_y[y, stat_rows : 2 * stat_rows] = picked
-    lse, picked = stat_round(stat_y, ny, y, 1, at_y)
-    stat_z[z, 0:stat_rows] = lse
-    stat_z[z, stat_rows : 2 * stat_rows] = picked
+    low_rows, high_rows = pl.ds(0, stat_rows), pl.ds(stat_rows, stat_rows)
+    rounds = (
+        (stat_x, nxc, xc, lambda i: at_x(i // NC, i % NC)),
+        (stat_y, ny, y, at_y),
+        (stat_z, nz, z, at_z),
+    )
+
+    def stat_send(k, some, out_sem, in_sem):
+        ref, n, me, device_of = rounds[k]
+        exchange(n, me, lambda i: ref.at[i, some], send_sem.at[out_sem + k], recv_sem.at[in_sem + k], device_of)
+
+    def picked_of(k):
+        ref, n = rounds[k][:2]
+        arrived(ref.at[0 : n - 1, high_rows], recv_sem.at[17 + k])
+        return sum(ref[i, stat_rows : 2 * stat_rows] for i in range(n))
 
     def settle():
         for i, ref in enumerate(
@@ -537,18 +533,31 @@
                 rows.at[:, :, :, :, all_a],
                 rows.at[:, :, :, :, all_b],
                 rows.at[:, :, :, :, all_c],
-                stat_x.at[0 : nxc - 1],
-                stat_y.at[0 : ny - 1],
             )
         ):
             left(ref, send_sem.at[i])
+        for k, (ref, n, _, _) in enumerate(rounds[:2]):
+            left(ref.at[0 : n - 1, low_rows], send_sem.at[15 + k])
+            left(ref.at[0 : n - 1, high_rows], send_sem.at[18 + k])
         rows_store.wait()
 
-    lse, picked = stat_round(stat_z, nz, z, 2, at_z, settle)
+    for k, (ref, n, me, _) in enumerate(rounds):
+        if k > 0:
+            ref[me, 0:stat_rows] = lse
+        stat_send(k, low_rows, 15, 10)
+        if k > 0:
+            ref[me, stat_rows : 2 * stat_rows] = picked_of(k - 1)
+        stat_send(k, high_rows, 18, 17)
+        if k == 2:
+            settle()
+        arrived(ref.at[0 : n - 1, low_rows], recv_sem.at[10 + k])
+        lses = [ref[i, 0:stat_rows] for i in range(n)]
+        top_ = functools.reduce(jnp.maximum, lses)
+        lse = top_ + jnp.log(sum(jnp.exp(s - top_) for s in lses))
 
     place = lax.broadcasted_iota(jnp.int32, lse.shape, 0) * 128 + lax.broadcasted_iota(jnp.int32, lse.shape, 1)
     live = place < tgt_len[0]
-    loss_out[...] = jnp.where(live, lse - picked, 0.0)
+    row_lse = lse
     lse = jnp.where(live, lse, 1e30)
     lse = jnp.concatenate([lse[r : r + 1, :] for r in range(stat_rows)], axis=1)
     place = lax.broadcasted_iota(jnp.int32, labels.shape, 1)
@@ -563,7 +572,9 @@
 
     lax.fori_loop(0, table_rows // 128, grad_step, 0)
 
-    left(stat_z.at[0 : nz - 1], send_sem.at[17])
+    loss_out[...] = jnp.where(live, row_lse - picked_of(2), 0.0)
+    left(stat_z.at[0 : nz - 1, low_rows], send_sem.at[17])
+    left(stat_z.at[0 : nz - 1, high_rows], send_sem.at[20])
     pltpu.make_async_copy(grad, grad_out, store_sem.at[1]).wait()
 
 
@@ -666,8 +677,8 @@
             dma((nz,)),
             dma((ny,)),
             dma((6,)),
-            dma((18,)),
-            dma((17,)),
+            dma((21,)),
+            dma((20,)),
         ],
         compiler_params=pltpu.CompilerParams(
             collective_id=0, has_side_effects=True, vmem_limit_bytes=40 * 1024 * 1024

time: 81.5 us -> 80.5 us (0.988)
  Pallas kernels: 79.5 us -> 78.4 us
    pallas_call x1, Pallas kernels: 5.56 us -> 4.62 us  [body(): pl.pallas_call(grad_kernel, out_shape=(jax.ShapeDtypeStruct((table_rows,...]
where the time goes in v7:
time: 80.5 us; the launch traced here: 80.3 us
  Pallas kernels  78.4 us (97%)
  between operations  1.93 us (2%)
    pallas_call x1, Pallas kernels, body(): pl.pallas_call(functools.partial(front_kernel, cfg), out_shape=(jax.Shape...  73.8 us
    pallas_call x1, Pallas kernels, body(): pl.pallas_call(grad_kernel, out_shape=(jax.ShapeDtypeStruct((table_rows,...  4.62 us

profile of v7, /device:TPU:1, one launch (start us, length us, event | category | flops | bytes accessed | tf_op | source)
XLA Modules:
  0.0 80.3 jit_solution(757257425890662246)
XLA Ops:
  1.9 73.8 %shard_map.122 = (f32[8,128]{1,0:T(8,128)S(1)}, bf16[896,1024]{1,0:T(8,128)(2,1)S(1)}, bf16[8,2,4,16,2048]{4,3,2,1,0:T(8,128)(2,1)S(1)}) custom-call(s32[1]{0:T(128)S(6)} %copy.13.src_len, s32[1]{0:T(128)S(6)} %copy.14.tgt_len, bf16[128,2048]{1,0:T(8,128)(2,1)} %dec_in.1, bf16[128,2048]{1,0:T(8,128)(2,1)} %enc_in.1, f32[2,2048]{1,0:T(2,128)} %gains_in.1, ...), custom_call_target="tpu_custom_call" | custom-call | tf_op jit(solution)/shard_map/pallas_call | solution.py:643
  75.7 4.6 %shard_map.123 = (bf16[896,2048]{1,0:T(8,128)(2,1)}, f32[8,128]{1,0:T(8,128)}) custom-call(s32[1]{0:T(128)S(6)} %copy.14.tgt_len, bf16[896,1024]{1,0:T(8,128)(2,1)S(1)} %get-tuple-element.7.grad, bf16[8,2,4,16,2048]{4,3,2,1,0:T(8,128)(2,1)S(1)} %get-tuple-element.8.rows, f32[8,128]{1,0:T(8,128)S(1)} %get-tuple-element.9.loss), custom_call_target="tpu_custom_call" | custom-call | tf_op jit(solution)/shard_map/pallas_call | solution.py:688

commit v8 on v7

--- a/solution.py
+++ b/solution.py
@@ -372,46 +372,65 @@
 
     mid = nz // 2
 
-    def half_x(i, part_):
-        return rows.at[part_ * mid : (part_ + 1) * mid, i // nxl, :, :, cols_piece(i % nxl)[2]]
-
-    def half_y(i, part_):
-        return rows.at[part_ * mid : (part_ + 1) * mid, :, i, :, all_c]
-
-    def relay_send(view, block, part_, sem, to, device_of):
-        ref = view(block, part_)
-        remote(ref, ref, send_sem.at[11], c_recv.at[sem], device_of(to)).start()
-
-    def relay_get(view, block, part_, sem):
-        ref = view(block, part_)
-        arrived(ref, c_recv.at[sem])
-        share(2, ref)
-
-    def relay_start(view, me, device_of):
+    def half_x(kind, i, part_):
+        return rows.at[part_ * mid : (part_ + 1) * mid, i // nxl, :, :, cols_piece(i % nxl)[kind]]
+
+    def half_y(kind, i, part_):
+        return rows.at[part_ * mid : (part_ + 1) * mid, :, i, :, cols_all(c)[kind]]
+
+    relay_sems = (None, b_recv, c_recv)
+
+    def relay_send(view, kind, block, part_, sem, to, device_of):
+        ref = view(kind, block, part_)
+        remote(ref, ref, send_sem.at[9 + kind], relay_sems[kind].at[sem], device_of(to)).start()
+
+    def relay_get(view, kind, block, part_, sem):
+        ref = view(kind, block, part_)
+        arrived(ref, relay_sems[kind].at[sem])
+        share(kind, ref)
+
+    def relay_start(view, kind, me, device_of):
         for first in (0, 1):
-            relay_send(view, me, first, first, (me + 1) % nx, device_of)
-            relay_send(view, me, 1 - first, 3 - first, (me + nx - 1) % nx, device_of)
+            relay_send(view, kind, me, first, first, (me + 1) % nx, device_of)
+            relay_send(view, kind, me, 1 - first, 3 - first, (me + nx - 1) % nx, device_of)
         for part_ in (0, 1):
-            share(2, view(me, part_))
-
-    def relay_pass(view, me, device_of):
+            share(kind, view(kind, me, part_))
+
+    def relay_pass(view, kind, me, device_of):
         down, up = (me + nx - 1) % nx, (me + 1) % nx
-        relay_get(view, down, 0, 0)
-        relay_send(view, down, 0, 4, up, device_of)
-        relay_get(view, up, 1, 3)
-        relay_send(view, up, 1, 5, down, device_of)
-
-    def relay_end(view, me):
-        relay_get(view, (me + nx - 1) % nx, 1, 1)
-        relay_get(view, (me + 1) % nx, 0, 2)
-        relay_get(view, (me + 2) % nx, 0, 4)
-        relay_get(view, (me + 2) % nx, 1, 5)
+        relay_get(view, kind, down, 0, 0)
+        relay_send(view, kind, down, 0, 4, up, device_of)
+        relay_get(view, kind, up, 1, 3)
+        relay_send(view, kind, up, 1, 5, down, device_of)
+
+    def relay_end(view, kind, me):
+        relay_get(view, kind, (me + nx - 1) % nx, 1, 1)
+        relay_get(view, kind, (me + 1) % nx, 0, 2)
+        relay_get(view, kind, (me + 2) % nx, 0, 4)
+        relay_get(view, kind, (me + 2) % nx, 1, 5)
 
     def slab(kind, z_):
         return rows.at[z_, :, :, :, all_a]
 
+    def a_post(block, o, device):
+        ref = slab(0, block)
+        remote(ref, ref, send_sem.at[9], a_recv.at[o], at_z(device)).start()
+
+    def a_get(o):
+        ref = slab(0, (z + o) % nz)
+        arrived(ref, a_recv.at[o])
+        share(0, ref)
+
+    def a_pass():
+        for o, next_o, device in ((2, 3, z + nz - 1), (nz - 2, nz - 3, z + 1)):
+            arrived(slab(0, (z + o) % nz), a_recv.at[o])
+            a_post((z + o) % nz, next_o, device % nz)
+            share(0, slab(0, (z + o) % nz))
+
     arrived(all_a1, recv_sem.at[4])
-    last(slab, 0, nz, z, a_recv, at_z)
+    for o in (2, nz - 2, 4, 1, nz - 1):
+        a_post(z, o, (z + nz - o) % nz)
+    share(0, slab(0, z))
     arrived(all_c1, recv_sem.at[6])
     ref = c2((x, y))
     for o in far_first(nx):
@@ -424,21 +443,26 @@
 
     @pl.when(c == 0)
     def _():
-        relay_start(half_x, x, at_x_)
+        relay_start(half_x, 2, x, at_x_)
         arrived(all_b2, recv_sem.at[15])
-        last(along_y, 1, ny, y, b_recv, at_y)
-        relay_pass(half_x, x, at_x_)
-        last_in(along_y, 1, ny, y, b_recv)
+        relay_start(half_y, 1, y, at_y)
+        a_pass()
+        relay_pass(half_x, 2, x, at_x_)
+        relay_pass(half_y, 1, y, at_y)
+        relay_end(half_y, 1, y)
 
     @pl.when(c == 1)
     def _():
-        relay_start(half_y, y, at_y)
+        relay_start(half_y, 2, y, at_y)
         arrived(all_b2, recv_sem.at[15])
-        last(along_x, 1, nx, x, b_recv, at_x_)
-        relay_pass(half_y, y, at_y)
-        last_in(along_x, 1, nx, x, b_recv)
-
-    last_in(slab, 0, nz, z, a_recv)
+        relay_start(half_x, 1, x, at_x_)
+        a_pass()
+        relay_pass(half_y, 2, y, at_y)
+        relay_pass(half_x, 1, x, at_x_)
+        relay_end(half_x, 1, x)
+
+    for o in (1, nz - 1, 4, 3, nz - 3):
+        a_get(o)
     their_a, their_b, their_c = cols_all(1 - c)
     arrived(rows.at[:, :, :, :, their_a], recv_sem.at[7])
     arrived(rows.at[:, :, :, :, their_b], recv_sem.at[8])
@@ -468,11 +492,11 @@
 
     @pl.when(c == 0)
     def _():
-        relay_end(half_x, x)
+        relay_end(half_x, 2, x)
 
     @pl.when(c == 1)
     def _():
-        relay_end(half_y, y)
+        relay_end(half_y, 2, y)
 
     lax.fori_loop(0, steps, early_step, 0)
     arrived(rows.at[:, :, :, :, their_c], recv_sem.at[9])
@@ -675,7 +699,7 @@
             dma((2,)),
             dma((2, half, 2)),
             dma((nz,)),
-            dma((ny,)),
+            dma((6,)),
             dma((6,)),
             dma((21,)),
             dma((20,)),

time: 80.5 us -> 80.4 us (level)
  no operation moved by 1% of the time
where the time goes in v8:
time: 80.4 us; the launch traced here: 79.9 us
  Pallas kernels  77.9 us (97%)
  between operations  1.93 us (2%)
    pallas_call x1, Pallas kernels, body(): pl.pallas_call(functools.partial(front_kernel, cfg), out_shape=(jax.Shape...  73.3 us
    pallas_call x1, Pallas kernels, body(): pl.pallas_call(grad_kernel, out_shape=(jax.ShapeDtypeStruct((table_rows,...  4.59 us

profile of v8, /device:TPU:1, one launch (start us, length us, event | category | flops | bytes accessed | tf_op | source)
XLA Modules:
  0.0 79.9 jit_solution(13251881815401921678)
XLA Ops:
  1.9 73.3 %shard_map.122 = (f32[8,128]{1,0:T(8,128)S(1)}, bf16[896,1024]{1,0:T(8,128)(2,1)S(1)}, bf16[8,2,4,16,2048]{4,3,2,1,0:T(8,128)(2,1)S(1)}) custom-call(s32[1]{0:T(128)S(6)} %copy.13.src_len, s32[1]{0:T(128)S(6)} %copy.14.tgt_len, bf16[128,2048]{1,0:T(8,128)(2,1)} %dec_in.1, bf16[128,2048]{1,0:T(8,128)(2,1)} %enc_in.1, f32[2,2048]{1,0:T(2,128)} %gains_in.1, ...), custom_call_target="tpu_custom_call" | custom-call | tf_op jit(solution)/shard_map/pallas_call | solution.py:667
  75.3 4.6 %shard_map.123 = (bf16[896,2048]{1,0:T(8,128)(2,1)}, f32[8,128]{1,0:T(8,128)}) custom-call(s32[1]{0:T(128)S(6)} %copy.14.tgt_len, bf16[896,1024]{1,0:T(8,128)(2,1)S(1)} %get-tuple-element.7.grad, bf16[8,2,4,16,2048]{4,3,2,1,0:T(8,128)(2,1)S(1)} %get-tuple-element.8.rows, f32[8,128]{1,0:T(8,128)S(1)} %get-tuple-element.9.loss), custom_call_target="tpu_custom_call" | custom-call | tf_op jit(solution)/shard_map/pallas_call | solution.py:712
